TPU v7x, 32 devices: a whole 2x2x4 slice. The times are simulated.
32 devices in a mesh: dp: 8 (over z, x), head: 4 (over y, core).
Axes of the slice: x: 2, y: 2, z: 4, core: 2. Of those that a mesh axis runs over, the one named last changes fastest.
Arguments:
- tokens: bfloat16 [32768, 768], P(('dp', 'head')), may hold values from -6 to 6
- cotangent: bfloat16 [32768, 768], P(('dp', 'head')), may hold values from -6 to 6
- lengths: int32 [32, 8], P('dp'), may hold values from 1 to 512, 1024 in all within a row
- masters: float32 [12, 768, 768], P(None, ('dp', 'head')), may hold values from -1 to 1
- vectors: float32 [12, 768], P(None, ('dp', 'head')), may hold values from -1.5 to 1.5
- left_stats: float32 [12, 768, 768], P(None, ('dp', 'head')), may hold values from -62914.56 to 254174.822, as said below
- right_stats: float32 [12, 768, 768], P(None, ('dp', 'head')), may hold values from -62914.56 to 254174.822, as said below
- vector_second: float32 [12, 768], P(None, ('dp', 'head')), may hold values from 163.84 to 1310.72
Outputs:
- output: bfloat16 [32768, 768], P(('dp', 'head'))
- input_grad: float32 [32768, 768], P(('dp', 'head'))
- block_grads: float32 [12, 768, 768], P(None, ('dp', 'head'))
- left_new: float32 [12, 768, 768], P(None, ('dp', 'head'))
- right_new: float32 [12, 768, 768], P(None, ('dp', 'head'))
- masters_new: float32 [12, 768, 768], P(None, ('dp', 'head'))
- vector_grads: float32 [12, 768], P(None, ('dp', 'head'))
- second_new: float32 [12, 768], P(None, ('dp', 'head'))
- vectors_new: float32 [12, 768], P(None, ('dp', 'head'))
Inputs may be any that keep to these rules, and one draw needn't show every extreme that they name: Row r of lengths lists, in order, the lengths of the documents packed into row r of 1024 tokens; each row sums to 1024. Each block of left_stats is symmetric. Each block of right_stats is symmetric.
All inputs are finite; a program needn't handle non-finite values.
Results may differ from a plain program's by a relative error of at most 0.012.
The roundings to bfloat16 on the way count: a program that leaves them out, or rounds other values in their place, can miss the bound.
Values may be sent and summed in bfloat16 or wider, within the bound.
A program may use at most 256 MiB of HBM per device.

v0:
```python
import jax, jax.numpy as jnp, numpy as np
from functools import partial
from jax import lax
from jax.experimental import pallas as pl
from jax.experimental.pallas import tpu as pltpu
from jax.sharding import PartitionSpec as P

D=768; HEADS=12; HD=64; FF=3072; PACK=1024; NEWTON=8; NB=12
NORM_EPS=1e-6
f32=jnp.float32; bf16=jnp.bfloat16
BIG=1e30
QB=256
def dot(a,b,ca=1,cb=0):
    return lax.dot_general(a,b,(((ca,),(cb,)),((),())),preferred_element_type=f32)

def doc_column(len_ref, shape, dim):
    t=lax.broadcasted_iota(jnp.int32,shape,dim)
    end=jnp.int32(0); doc=jnp.zeros(shape,jnp.int32)
    for j in range(8):
        end=end+len_ref[0,j]
        doc=doc+(t>=end).astype(jnp.int32)
    return doc

def split3(v):
    a=v.astype(bf16).astype(f32); r=v-a
    b=r.astype(bf16).astype(f32); c=r-b
    return a,b,c

def augment(base, lane, head_lo, cols):
    keep=(lane<64) if head_lo else (lane>=64)
    off=64 if head_lo else 0
    out=jnp.where(keep, base, 0.0)
    for i,c in enumerate(cols):
        out=jnp.where(lane==off+i, c, out)
    return out.astype(bf16)

def onehot_part(base, lane, head_lo, doc, minus, scale):
    keep=(lane<64) if head_lo else (lane>=64)
    off=64 if head_lo else 0
    l=lane-off
    oh=jnp.where((l>=0)&(l<8), (jnp.where(l==doc,1.0,0.0)-minus)*scale, 0.0)
    return jnp.where(keep, base, oh)

def attn_fwd_pair(p, q_ref,k_ref,v_ref, ctx_ref, lse_ref, doc):
    cols=pl.ds(pl.multiple_of(p*128,128),128)
    lane=lax.broadcasted_iota(jnp.int32,(PACK,128),1)
    kp=k_ref[:,cols].astype(f32)
    vp=v_ref[:,cols]
    kk=[onehot_part(kp,lane,lo,doc,1.0,1.0).astype(bf16) for lo in (True,False)]
    laneb=lax.broadcasted_iota(jnp.int32,(QB,128),1)
    for b in range(PACK//QB):
        rows=pl.ds(b*QB,QB)
        qp=q_ref[rows,cols].astype(f32)*0.125
        docb=doc[b*QB:(b+1)*QB]
        outs=[]
        lse_old=lse_ref[rows,:]
        for h,lo in enumerate((True,False)):
            qa=onehot_part(qp,laneb,lo,docb,0.0,BIG).astype(bf16)
            s=dot(qa,kk[h],1,1)
            m=jnp.max(s,axis=1,keepdims=True)
            e=jnp.exp(s-m)
            l=jnp.sum(e,axis=1,keepdims=True)
            o=dot(e.astype(bf16),vp)
            outs.append(o/l)
            lse_old=jnp.where(laneb==2*p+h, m+jnp.log(l), lse_old)
        lse_ref[rows,:]=lse_old
        ctx_ref[rows,cols]=jnp.where(laneb<64,outs[0],outs[1]).astype(bf16)

def layer_norm(z):
    mu=jnp.mean(z,axis=-1,keepdims=True)
    c=z-mu
    r=lax.rsqrt(jnp.mean(c*c,axis=-1,keepdims=True)+NORM_EPS)
    return c*r, r

def ka_body(len_ref,x_ref,wa_ref,p_ref,q_ref,k_ref,v_ref,ctx_ref,lse_ref,hid_ref,r1_ref,w_ref):
    pltpu.sync_copy(wa_ref.at[pl.ds(0,4)],w_ref)
    doc=doc_column(len_ref,(PACK,1),0)
    for i,(o,b) in enumerate(((q_ref,0),(k_ref,None),(v_ref,1))):
        for t in range(4):
            rows=pl.ds(t*256,256)
            y=dot(x_ref[rows,:],w_ref[i])
            if b is not None: y=y+p_ref[b:b+1,:]
            o[rows,:]=y.astype(bf16)
    def body(p,c):
        attn_fwd_pair(p,q_ref,k_ref,v_ref,ctx_ref,lse_ref,doc)
        return c
    lax.fori_loop(0,6,body,0)
    for t in range(4):
        rows=pl.ds(t*256,256)
        z=x_ref[rows,:].astype(f32)+(dot(ctx_ref[rows,:],w_ref[3])+p_ref[2:3,:])
        n,r=layer_norm(z)
        hid_ref[rows,:]=n
        r1_ref[rows,:]=jnp.broadcast_to(r,(256,128))

def call_a(lengths,x,w,params):
    V=pltpu.VMEM
    return pl.pallas_call(ka_body,
        in_specs=[pl.BlockSpec(memory_space=pltpu.SMEM),pl.BlockSpec(memory_space=V),pl.BlockSpec(memory_space=pl.ANY),pl.BlockSpec(memory_space=V)],
        out_specs=[pl.BlockSpec(memory_space=V)]*7,
        out_shape=[jax.ShapeDtypeStruct((PACK,D),bf16)]*4+[jax.ShapeDtypeStruct((PACK,128),f32),jax.ShapeDtypeStruct((PACK,D),f32),jax.ShapeDtypeStruct((PACK,128),f32)],
        scratch_shapes=[V((4,D,D),bf16)],
        compiler_params=pltpu.CompilerParams(vmem_limit_bytes=60<<20))(lengths,x,w,params)

def gelu_both(x):
    z=jnp.abs(x)*0.7071067811865476
    t=1.0/(1.0+0.3275911*z)
    e=jnp.exp(-0.5*x*x)
    poly=t*(0.254829592+t*(-0.284496736+t*(1.421413741+t*(-1.453152027+t*1.061405429))))
    half=0.5*poly*e
    phi_c=jnp.where(x>=0,1.0-half,half)
    return x*phi_c, phi_c+x*(e*0.3989422804014327)

def kb_body(cot_ref,n1_ref,r1_ref,ctx_ref,w_ref,p_ref, out_ref,dz1_ref,dctx_ref,dwo_ref,dw1_ref,dw2_ref,vec_ref, act_ref,gp_ref,dffn_ref,hlow_ref):
    TT=256
    g1,s1,g2,s2=(p_ref[i:i+1,:] for i in (8,9,10,11))
    b2=p_ref[7:8,:]
    vec_ref[...]=jnp.zeros_like(vec_ref)
    def tile(t,carry):
        rows=pl.ds(pl.multiple_of(t*TT,TT),TT)
        n1=n1_ref[rows,:]
        hid=n1*g1+s1
        hl=hid.astype(bf16)
        hlow_ref[rows,:]=hl
        ffn=None
        for c in range(4):
            inner=dot(hl,w_ref[4+c])+p_ref[3+c:4+c,:]
            a,gp=gelu_both(inner)
            al=a.astype(bf16)
            act_ref[rows,pl.ds(c*D,D)]=al
            gp_ref[rows,pl.ds(c*D,D)]=gp.astype(gp_ref.dtype)
            y=dot(al,w_ref[8+c])
            ffn=y if ffn is None else ffn+y
        z=hid+(ffn+b2)
        n2,r2=layer_norm(z)
        out_ref[rows,:]=(n2*g2+s2).astype(bf16)
        e=cot_ref[rows,:].astype(f32)
        c2=e*g2
        dz2=r2*(c2-jnp.mean(c2,axis=-1,keepdims=True)-n2*jnp.mean(c2*n2,axis=-1,keepdims=True))
        dffn=dz2.astype(bf16)
        dffn_ref[rows,:]=dffn
        vec_ref[10:11,:]+=jnp.sum(e*n2,axis=0,keepdims=True)
        vec_ref[11:12,:]+=jnp.sum(e,axis=0,keepdims=True)
        vec_ref[7:8,:]+=jnp.sum(dffn.astype(f32),axis=0,keepdims=True)
        dh=dz2
        for c in range(4):
            dact=dot(dffn,w_ref[8+c],1,1)
            din=(dact*gp_ref[rows,pl.ds(c*D,D)].astype(f32)).astype(bf16)
            gp_ref[rows,pl.ds(c*D,D)]=din.astype(gp_ref.dtype)
            vec_ref[3+c:4+c,:]+=jnp.sum(din.astype(f32),axis=0,keepdims=True)
            dh=dh+dot(din,w_ref[4+c],1,1)
        vec_ref[8:9,:]+=jnp.sum(dh*n1,axis=0,keepdims=True)
        vec_ref[9:10,:]+=jnp.sum(dh,axis=0,keepdims=True)
        c1=dh*g1
        dz1=r1_ref[rows,0:1]*(c1-jnp.mean(c1,axis=-1,keepdims=True)-n1*jnp.mean(c1*n1,axis=-1,keepdims=True))
        dz1_ref[rows,:]=dz1
        dat=dz1.astype(bf16)
        vec_ref[2:3,:]+=jnp.sum(dat.astype(f32),axis=0,keepdims=True)
        dctx_ref[rows,:]=dot(dat,w_ref[3],1,1).astype(bf16)
        return carry
    lax.fori_loop(0,PACK//TT,tile,0)
    for c in range(4):
        dw2_ref[c]=dot(act_ref[:,c*D:(c+1)*D],dffn_ref[...],0,0).astype(bf16)
        dw1_ref[c]=dot(hlow_ref[...],gp_ref[:,c*D:(c+1)*D].astype(bf16),0,0).astype(bf16)
    dwo_ref[...]=dot(ctx_ref[...],dz1_ref[...].astype(bf16),0,0).astype(bf16)

def call_b(cot,n1,r1,ctx,w,params):
    V=pltpu.VMEM
    S=jax.ShapeDtypeStruct
    return pl.pallas_call(kb_body,
        in_specs=[pl.BlockSpec(memory_space=V)]*6,
        out_specs=[pl.BlockSpec(memory_space=V)]*7,
        out_shape=[S((PACK,D),bf16),S((PACK,D),f32),S((PACK,D),bf16),S((D,D),bf16),S((4,D,D),bf16),S((4,D,D),bf16),S((16,D),f32)],
        scratch_shapes=[V((PACK,FF),bf16),V((PACK,FF),bf16),V((PACK,D),bf16),V((PACK,D),bf16)],
        compiler_params=pltpu.CompilerParams(vmem_limit_bytes=62<<20))(cot,n1,r1,ctx,w,params)

def kc_body(len_ref,x_ref,q_ref,k_ref,v_ref,ctx_ref,do_ref,lse_ref,dz1_ref,wa_ref, ig_ref,dw_ref,vec_ref, dqkv_ref, dqa_ref,w_ref):
    pltpu.sync_copy(wa_ref.at[pl.ds(0,3)],w_ref)
    doc=doc_column(len_ref,(PACK,1),0)
    lane=lax.broadcasted_iota(jnp.int32,(PACK,128),1)
    KB_=256
    def pair(p,carry):
        cols=pl.ds(pl.multiple_of(p*128,128),128)
        qp=q_ref[:,cols].astype(f32); kp=k_ref[:,cols].astype(f32); vp=v_ref[:,cols].astype(f32)
        dop=do_ref[:,cols].astype(f32); cp=ctx_ref[:,cols].astype(f32)
        prod=dop*cp
        qa=[];qm=[];doa=[];dom=[];ka=[];km=[];va=[]
        for h,lo in enumerate((True,False)):
            keep=(lane<64) if lo else (lane>=64)
            off=64 if lo else 0
            lse=jnp.sum(jnp.where(lane==2*p+h,lse_ref[...],0.0),axis=1,keepdims=True)
            dd=jnp.sum(jnp.where(keep,prod,0.0),axis=1,keepdims=True)
            q1=onehot_part(qp*0.125,lane,lo,doc,0.0,BIG)
            for i,c in enumerate(split3(-lse)): q1=jnp.where(lane==off+8+i,c,q1)
            qa.append(q1.astype(bf16)); qm.append(jnp.where(keep,qp*0.125,0.0).astype(bf16))
            k1=onehot_part(kp,lane,lo,doc,1.0,1.0)
            k1=jnp.where((lane>=off+8)&(lane<off+11),1.0,k1)
            ka.append(k1.astype(bf16)); km.append(jnp.where(keep,kp*0.125,0.0).astype(bf16))
            d1=jnp.where(keep,dop,0.0)
            dom.append(d1.astype(bf16))
            for i,c in enumerate(split3(-dd)): d1=jnp.where(lane==off+i,c,d1)
            doa.append(d1.astype(bf16))
            v1=jnp.where(keep,vp,0.0); v1=jnp.where((lane>=off)&(lane<off+3),1.0,v1)
            va.append(v1.astype(bf16))
        for b in range(PACK//KB_):
            rows=slice(b*KB_,(b+1)*KB_)
            dv=None;dk=None;dq=None
            for h in range(2):
                s=dot(ka[h][rows],qa[h],1,1)
                pr=jnp.exp(s)
                dp=dot(va[h][rows],doa[h],1,1)
                ds=(pr*dp).astype(bf16)
                a=dot(pr.astype(bf16),dom[h]); dv=a if dv is None else dv+a
                a=dot(ds,qm[h]); dk=a if dk is None else dk+a
                a=dot(ds,km[h][rows],0,0); dq=a if dq is None else dq+a
            if b==0: dqa_ref[...]=dq
            else: dqa_ref[...]+=dq
            dqkv_ref[1,rows,cols]=dk.astype(bf16)
            dqkv_ref[2,rows,cols]=dv.astype(bf16)
        dqkv_ref[0,:,cols]=dqa_ref[...].astype(bf16)
        for i in range(3):
            d=dqkv_ref[i,:,cols]
            dw_ref[i,:,cols]=dot(x_ref[...],d,0,0).astype(bf16)
            vec_ref[i:i+1,cols]=jnp.sum(d.astype(f32),axis=0,keepdims=True)
        return carry
    lax.fori_loop(0,6,pair,0)
    for t in range(4):
        rows=pl.ds(t*256,256)
        acc=dz1_ref[rows,:]
        for i in range(3):
            acc=acc+dot(dqkv_ref[i,rows,:],w_ref[i],1,1)
        ig_ref[rows,:]=acc

def call_c(lengths,x,q,k,v,ctx,do,lse,dz1,w):
    V=pltpu.VMEM; S=jax.ShapeDtypeStruct
    return pl.pallas_call(kc_body,
        in_specs=[pl.BlockSpec(memory_space=pltpu.SMEM)]+[pl.BlockSpec(memory_space=V)]*8+[pl.BlockSpec(memory_space=pl.ANY)],
        out_specs=[pl.BlockSpec(memory_space=V)]*3,
        out_shape=[S((PACK,D),f32),S((3,D,D),bf16),S((8,D),f32)],
        scratch_shapes=[V((3,PACK,D),bf16),V((PACK,128),f32),V((3,D,D),bf16)],
        compiler_params=pltpu.CompilerParams(vmem_limit_bytes=62<<20))(lengths,x,q,k,v,ctx,do,lse,dz1,w)

RB=256
def diag_sum(blk):
    i=lax.broadcasted_iota(jnp.int32,blk.shape,0); j=lax.broadcasted_iota(jnp.int32,blk.shape,1)
    return jnp.sum(jnp.where(i==j,blk,0.0),keepdims=True)
def eye_rows(rb):
    i=lax.broadcasted_iota(jnp.int32,(RB,D),0)+rb*RB; j=lax.broadcasted_iota(jnp.int32,(RB,D),1)
    return i==j
def newton(m_ref,x_ref,nb_ref,pb_ref,sb_ref,xb_ref):
    nblk=D//RB
    R=[slice(i*RB,(i+1)*RB) for i in range(nblk)]
    tot=jnp.zeros((1,1),f32); tr=jnp.zeros((1,1),f32)
    for i in range(nblk):
        blk=m_ref[R[i],:]
        tot=tot+jnp.sum(blk*blk,keepdims=True)
        tr=tr+diag_sum(blk[:,R[i]])
    c=jnp.sqrt(tot+1e-6)
    inv=1.0/c
    al=tr*inv/D
    s=lax.rsqrt(jnp.sqrt(c))
    for i in range(nblk):
        m_ref[R[i],:]=m_ref[R[i],:]*inv
    def iteration(k,al,be,first=False,last=False):
        u=5-al
        u2=u*u;u3=u2*u;u4=u2*u2
        c0=al*u4*(1/256); c1=(u4-4*al*u3)*(1/256); c2=(12*al*u2-8*u3)*(1/512)
        c3=(36*u2-24*al*u)*(1/1536); c4=(24*al-96*u)*(1/6144); c5=1/256
        for i in range(nblk):
            nb_ref[R[i],:]=jnp.where(eye_rows(i),m_ref[R[i],:]-al,m_ref[R[i],:]).astype(bf16)
            if not first: xb_ref[R[i],:]=jnp.where(eye_rows(i),x_ref[R[i],:]-be,x_ref[R[i],:]).astype(bf16)
        be2=jnp.zeros((1,1),f32); al2=jnp.zeros((1,1),f32)
        for i in range(nblk):
            n=jnp.where(eye_rows(i),m_ref[R[i],:]-al,m_ref[R[i],:])
            if not last:
                p=dot(nb_ref[R[i],:],nb_ref[...])
                pb_ref[R[i],:]=p.astype(bf16)
                m=c1*n+c2*p
                m_ref[R[i],:]=jnp.where(eye_rows(i),m+c0,m)
            if first:
                x=jnp.where(eye_rows(i),1.25-al*0.25,0.0)-0.25*n
            else:
                x=(1.25-al*0.25)*x_ref[R[i],:]-0.25*(be*n+dot(xb_ref[R[i],:],nb_ref[...]))
            x_ref[R[i],:]=x
            be2=be2+diag_sum(x[:,R[i]])
        if not last:
            for i in range(nblk):
                q=dot(nb_ref[R[i],:],pb_ref[...])
                sb_ref[R[i],:]=(c3*nb_ref[R[i],:].astype(f32)+c4*pb_ref[R[i],:].astype(f32)+c5*q).astype(bf16)
            for i in range(nblk):
                m=m_ref[R[i],:]+dot(pb_ref[R[i],:],sb_ref[...])
                m_ref[R[i],:]=m
                al2=al2+diag_sum(m[:,R[i]])
        return al2*(1/D),be2*(1/D)
    al,be=iteration(0,al,None,first=True)
    al,be=lax.fori_loop(1,7,lambda k,ab:iteration(k,*ab),(al,be))
    iteration(7,al,be,last=True)
    for i in range(nblk):
        x_ref[R[i],:]=x_ref[R[i],:]*s
def body(a_ref,x_ref,m_ref,nb,pb,sb,xb):
    m_ref[...]=a_ref[...]
    newton(m_ref,x_ref,nb,pb,sb,xb)
def call_newton(a):
    V=pltpu.VMEM
    return pl.pallas_call(body,in_specs=[pl.BlockSpec(memory_space=V)],out_specs=pl.BlockSpec(memory_space=V),
      out_shape=jax.ShapeDtypeStruct((D,D),f32),scratch_shapes=[V((D,D),f32)]+[V((D,D),bf16)]*4,
      compiler_params=pltpu.CompilerParams(vmem_limit_bytes=60<<20))(a)

NZ=4; MR=48; HC=384
MESH=pl.DeviceIdType.MESH
def rcopy(src,dst,ss,rs,dev):
    return pltpu.make_async_remote_copy(src_ref=src,dst_ref=dst,send_sem=ss,recv_sem=rs,device_id=dev,device_id_type=MESH)

class Place:
    def __init__(self):
        self.dp=lax.axis_index("dp"); self.head=lax.axis_index("head")
        self.z=self.dp//2; self.x=self.dp%2; self.y=self.head//2; self.c=self.head%2
        self.xy=self.x*2+self.y
        self.chip=self.z*4+self.xy
        self.me=self.dp*4+self.head
        self.xn=((self.dp//2)*2+(1-self.x), self.head)
        self.yn=(self.dp,(1-self.y)*2+self.c)
        self.sib=(self.dp,self.y*2+(1-self.c))
        self.cols=pl.ds(pl.multiple_of(self.c*HC,128),HC)
        self.ocols=pl.ds(pl.multiple_of((1-self.c)*HC,128),HC)
    def zpeer(self,k):
        return (((self.z+k)%NZ)*2+self.x,self.head)
    def zfrom(self,k):
        return (self.z+NZ-k)%NZ
    def neighbours(self):
        return [self.zpeer(1),self.zpeer(2),self.zpeer(3),self.xn,self.yn,self.sib]

def greet(devs):
    bar=pltpu.get_barrier_semaphore()
    for d in devs:
        pl.semaphore_signal(bar,inc=1,device_id=d,device_id_type=MESH)
    pl.semaphore_wait(bar,len(devs))

def greet_all(pc):
    bar=pltpu.get_barrier_semaphore()
    def sig(k,carry):
        t=(pc.me+k)%32
        pl.semaphore_signal(bar,inc=1,device_id=(t//4,t%4),device_id_type=MESH)
        return carry
    lax.fori_loop(1,32,sig,0)
    pl.semaphore_wait(bar,31)

class Gather:
    def __init__(self,pc,buf,ss,rs):
        self.pc,self.buf,self.ss,self.rs=pc,buf,ss,rs
    def region(self,z,xy,mine=True):
        pc=self.pc
        return self.buf.at[z,xy,:,pc.cols if mine else pc.ocols]
    def copies(self):
        pc=self.pc; al=pl.ds(0,4); lo=pl.ds(0,2); hi=pl.ds(2,2)
        xo=(1-pc.x)*2+pc.y; yo=pc.x*2+(1-pc.y); dg=(1-pc.x)*2+(1-pc.y)
        R=self.region
        def mk(i,src,dst,dev):
            return rcopy(src,dst,self.ss.at[i],self.rs.at[i],dev)
        send={}
        for k in (1,2,3): send[k-1]=(R(pc.z,pc.xy),pc.zpeer(k))
        send[3]=(R(al,pc.xy),pc.xn); send[4]=(R(al,pc.xy),pc.yn)
        send[5]=(R(hi,yo),pc.xn); send[6]=(R(lo,xo),pc.yn)
        send[7]=(R(al,pc.xy),pc.sib); send[8]=(R(al,xo),pc.sib); send[9]=(R(al,yo),pc.sib); send[10]=(R(al,dg),pc.sib)
        recv={}
        for k in (1,2,3): recv[k-1]=R(pc.zfrom(k),pc.xy)
        recv[3]=R(al,xo); recv[4]=R(al,yo); recv[5]=R(hi,dg); recv[6]=R(lo,dg)
        recv[7]=R(al,pc.xy,False); recv[8]=R(al,xo,False); recv[9]=R(al,yo,False); recv[10]=R(al,dg,False)
        self.send=[partial(mk,i,send[i][0],send[i][0],send[i][1]) for i in range(11)]
        self.recv=[partial(mk,i,recv[i],recv[i],pc.sib) for i in range(11)]
        return self
    def step0(self):
        for i in (0,1,2): self.send[i]().start()
    def step1(self):
        for i in (0,1,2): self.recv[i]().wait_recv()
        for i in (3,4,7): self.send[i]().start()
    def step2(self):
        self.recv[3]().wait_recv()
        for i in (6,8): self.send[i]().start()
        self.recv[4]().wait_recv()
        for i in (5,9): self.send[i]().start()
    def step3(self):
        for i in (5,6): self.recv[i]().wait_recv()
        self.send[10]().start()
    def step4(self):
        for i in (7,8,9,10): self.recv[i]().wait_recv()
    def done(self):
        for i in range(11): self.send[i]().wait_send()
    def step(self,i):
        (self.step0,self.step1,self.step2,self.step3,self.step4)[i]()

ORDER=(0,1,2,3,4,8,5,9,6,10,7,11)
def ag_body(mas_ref,pv_ref,left_ref,right_ref, w_ref,pg_ref,st_ref, sibm,ss,rs,cs,cr,ts,tr,lsem):
    pc=Place()
    greet_all(pc)
    half=rcopy(mas_ref.at[:,:,pc.ocols],sibm,cs,cr,pc.sib)
    half.start()
    def stat(b,act):
        t=(b%4)*4+b//4
        for side,ref in enumerate((left_ref,right_ref)):
            dev=((t//2),(t%2)*2+side)
            idx=b*2+side
            mine=(pc.chip==t)&(pc.c==side)
            act(idx,ref.at[b],dev,mine)
    half.wait_recv()
    lo=pl.ds(0,24); hi=pl.ds(24,24)
    for b in ORDER:
        own=mas_ref[b,:,pc.cols]; oth=sibm[b]
        first=jnp.where(pc.c==0,own,oth); second=jnp.where(pc.c==0,oth,own)
        w_ref[b,pc.z,pc.xy,:,pc.cols]=jnp.concatenate([first,second],axis=0).astype(bf16)
    pg_ref[pc.z,pc.xy,:,pc.cols]=pv_ref[...]
    half.wait_send()
    gs=[Gather(pc,pg_ref,ss.at[12],rs.at[12]).copies()]+[Gather(pc,w_ref.at[b],ss.at[b],rs.at[b]).copies() for b in ORDER]
    for t in range(len(gs)+4):
        for s in range(5):
            if 0<=t-s<len(gs): gs[t-s].step(s)
    def start(b,carry):
        def act(idx,src,dev,mine):
            @pl.when(mine)
            def _(): pltpu.make_async_copy(src,st_ref.at[pc.me],tr).start()
            @pl.when(jnp.logical_not(mine))
            def _(): rcopy(src,st_ref.at[pc.me],ts.at[idx],tr,dev).start()
        stat(b,act)
        return carry
    lax.fori_loop(0,NB,start,0)
    for g in gs: g.done()
    def fin(b,carry):
        def act(idx,src,dev,mine):
            @pl.when(jnp.logical_not(mine))
            def _(): rcopy(src,st_ref.at[pc.me],ts.at[idx],tr,dev).wait_send()
        stat(b,act)
        return carry
    lax.fori_loop(0,NB,fin,0)
    @pl.when(pc.xy<3)
    def _(): pltpu.make_async_copy(st_ref,st_ref,tr).wait()

def call_ag(masters,pv,left,right):
    V=pltpu.VMEM; S=jax.ShapeDtypeStruct; A=pl.ANY
    B=lambda m: pl.BlockSpec(memory_space=m)
    sem=pltpu.SemaphoreType.DMA
    return pl.pallas_call(ag_body,in_specs=[B(V),B(V),B(A),B(A)],out_specs=[B(V),B(V),B(A)],
        out_shape=[S((NB,4,4,MR,D),bf16),S((4,4,16,D),bf16),S((32,24,D),f32)],
        scratch_shapes=[V((NB,24,HC),f32),sem((13,11)),sem((13,11)),sem,sem,sem((24,)),sem,sem],
        compiler_params=pltpu.CompilerParams(vmem_limit_bytes=60<<20,collective_id=0,has_side_effects=True))(masters,pv,left,right)

def params_of(pg):
    t=pg.reshape(16,16,2,HC)[:,:12,:,:24]
    return jnp.transpose(t,(1,0,2,3)).reshape(12,D).astype(f32)


class Scatter:
    def __init__(self,pc,b,g_ref,R,out_ref,gown_ref,ss,rs,os_,orr):
        self.pc,self.b,self.g=pc,b,g_ref.at[b]
        self.out,self.gown=out_ref,gown_ref
        self.os_,self.orr=os_,orr
        self.R={k:v.at[b] for k,v in R.items()}
        R=self.R
        s1,rc=R["s1"],R["rc"]
        def mk(i,src,dst,dev): return rcopy(src,dst,ss.at[b,i],rs.at[b,i],dev)
        lo=pl.ds(0,2); hi=pl.ds(2,2); al=pl.ds(0,4)
        self.core=mk(0,self.g.at[:,:,:,pc.ocols],rc,pc.sib)
        self.xa=mk(1,s1.at[lo,pl.ds((1-pc.x)*2,2)],R["xa"],pc.xn)
        self.yb=[mk(2+i,s1.at[hi,i*2+1-pc.y],R["yb"].at[i],pc.yn) for i in range(2)]
        self.ya=mk(4,R["s2a"],R["ya"],pc.yn)
        self.xb=mk(5,R["s2b"],R["xb"],pc.xn)
        self.zz=[mk(6+k-1,R["s3"].at[(pc.z+k)%NZ],R["zr"].at[k-1],pc.zpeer(k)) for k in (1,2,3)]
        self.home=mk(9,R["fin"].at[pl.ds(pl.multiple_of((1-pc.c)*24,8),24)],R["hr"],pc.sib)
        t=(b%4)*4+b//4
        self.t=t
        self.owner=[((t//2),(t%2)*2+side) for side in range(2)]
        self.to_owner=[rcopy(R["finb"],gown_ref.at[pc.chip,:,pc.cols],os_.at[b,side],orr,self.owner[side]) for side in range(2)]
        self.to_self=pltpu.make_async_copy(R["finb"],gown_ref.at[pc.chip,:,pc.cols],orr)
    def step0(self):
        self.core.start()
    def step1(self):
        pc=self.pc; R=self.R
        self.core.wait_recv()
        for z in range(4):
            R["s1"][z]=(self.g[z,:,:,pc.cols].astype(f32)+R["rc"][z].astype(f32)).astype(bf16)
        self.xa.start()
        for d in self.yb: d.start()
    def step2(self):
        pc=self.pc; R=self.R
        self.xa.wait_recv()
        s=R["s1"][0:2,pl.ds(pc.x*2,2)].astype(f32)+R["xa"][...].astype(f32)
        keep=jnp.where(pc.y==0,s[:,0],s[:,1]); give=jnp.where(pc.y==0,s[:,1],s[:,0])
        R["k2"][0:2]=keep; R["s2a"][...]=give.astype(bf16)
        self.ya.start()
        for d in self.yb: d.wait_recv()
        s0=R["s1"][2:4,pc.y].astype(f32)+R["yb"][0].astype(f32)
        s1=R["s1"][2:4,2+pc.y].astype(f32)+R["yb"][1].astype(f32)
        keep=jnp.where(pc.x==0,s0,s1); give=jnp.where(pc.x==0,s1,s0)
        R["k2"][2:4]=keep; R["s2b"][...]=give.astype(bf16)
        self.xb.start()
    def step3(self):
        R=self.R
        self.ya.wait_recv(); self.xb.wait_recv()
        a=R["k2"][0:2]+R["ya"][...].astype(f32)
        b=R["k2"][2:4]+R["xb"][...].astype(f32)
        R["k2"][0:2]=a; R["k2"][2:4]=b
        R["s3"][0:2]=a.astype(bf16); R["s3"][2:4]=b.astype(bf16)
        for d in self.zz: d.start()
    def step4(self):
        pc=self.pc; R=self.R
        for d in self.zz: d.wait_recv()
        s=R["k2"][pc.z]
        for k in range(3): s=s+R["zr"][k].astype(f32)
        R["fin"][...]=s
        R["finb"][...]=s.astype(bf16)
        self.home.start()
        @pl.when(pc.chip==self.t)
        def _():
            self.to_self.start()
            for side in range(2):
                @pl.when(pc.c!=side)
                def _(): self.to_owner[side].start()
        @pl.when(pc.chip!=self.t)
        def _():
            for d in self.to_owner: d.start()
    def step5(self):
        pc=self.pc; R=self.R
        self.home.wait_recv()
        own=R["fin"][pl.ds(pl.multiple_of(pc.c*24,8),24)]; oth=R["hr"][...]
        self.out[self.b,:,pc.cols]=own
        self.out[self.b,:,pc.ocols]=oth
    def step(self,i): (self.step0,self.step1,self.step2,self.step3,self.step4,self.step5)[i]()
    def done(self):
        pc=self.pc
        for d in [self.core,self.xa,*self.yb,self.ya,self.xb,*self.zz,self.home]: d.wait_send()
        @pl.when(pc.chip==self.t)
        def _():
            for side in range(2):
                @pl.when(pc.c!=side)
                def _(): self.to_owner[side].wait_send()
        @pl.when(pc.chip!=self.t)
        def _():
            for d in self.to_owner: d.wait_send()

def scatter_scratch(nb=NB):
    V=pltpu.VMEM
    return dict(s1=V((nb,4,4,MR,HC),bf16),rc=V((nb,4,4,MR,HC),bf16),xa=V((nb,2,2,MR,HC),bf16),yb=V((nb,2,2,MR,HC),bf16),
        s2a=V((nb,2,MR,HC),bf16),s2b=V((nb,2,MR,HC),bf16),ya=V((nb,2,MR,HC),bf16),xb=V((nb,2,MR,HC),bf16),
        k2=V((nb,4,MR,HC),f32),s3=V((nb,4,MR,HC),bf16),zr=V((nb,3,MR,HC),bf16),fin=V((nb,MR,HC),f32),finb=V((nb,MR,HC),bf16),hr=V((nb,24,HC),f32))

class VecSum:
    def __init__(self,pc,cur,buf,ss,rs):
        self.pc,self.cur,self.buf=pc,cur,buf
        zp=lambda bit: ((pc.z^bit)*2+pc.x,pc.head)
        z1=(pc.z+1-2*(pc.z%2)); z2=(pc.z+2)%4
        partners=[pc.sib,pc.xn,pc.yn,(z1*2+pc.x,pc.head),(z2*2+pc.x,pc.head)]
        self.d=[rcopy(cur.at[i],buf.at[i],ss.at[i],rs.at[i],p) for i,p in enumerate(partners)]
    def step(self,i):
        if i>0:
            self.d[i-1].wait_recv()
            self.cur[i]=self.cur[i-1]+self.buf[i-1]
        if i<5: self.d[i].start()
    def done(self):
        for d in self.d: d.wait_send()

RSORDER=(8,4,9,5,10,6,11,7,3,2,1,0)
KEYS=list(scatter_scratch())
def rs_body(g_ref,vec_ref,out_ref,vout_ref,gown_ref,*rest):
    R=dict(zip(KEYS,rest[:len(KEYS)])); vcur,vbuf,ss,rs,os_,orr,vs,vr=rest[len(KEYS):]
    pc=Place()
    greet_all(pc)
    vcur[0]=vec_ref[...]
    vsum=VecSum(pc,vcur,vbuf,vs,vr)
    sc=[Scatter(pc,b,g_ref,R,out_ref,gown_ref,ss,rs,os_,orr) for b in RSORDER]
    for t in range(len(sc)+5):
        for s in range(6):
            if 0<=t-s<len(sc): sc[t-s].step(s)
        if t<=5: vsum.step(t)
    vout_ref[...]=vcur[5]
    for s in sc: s.done()
    vsum.done()
    @pl.when(pc.xy<3)
    def _(): pltpu.make_async_copy(gown_ref,gown_ref,orr).wait()

def call_rs(g,vec):
    V=pltpu.VMEM; S=jax.ShapeDtypeStruct
    B=pl.BlockSpec(memory_space=V); sem=pltpu.SemaphoreType.DMA
    return pl.pallas_call(rs_body,in_specs=[B,B],out_specs=[B,B,B],
        out_shape=[S((NB,24,D),f32),S((16,D),f32),S((16,MR,D),bf16)],
        scratch_shapes=list(scatter_scratch().values())+[V((6,16,D),f32),V((5,16,D),f32),sem((NB,10)),sem((NB,10)),sem((NB,2)),sem,sem((5,)),sem((5,))],
        compiler_params=pltpu.CompilerParams(vmem_limit_bytes=62<<20,collective_id=1,has_side_effects=True))(g,vec)

BETA=0.95; BETA_TWO=0.99; RATE=1.0; RATE_VEC=0.05

def owner_of(b):
    return ((b//3+(b%3)%2+1)%4)*4+b%3
def owned_by(pc):
    return 3*((pc.z+3-pc.xy%2)%4)+pc.xy

def pack(rows):
    return jnp.concatenate([rows[:,:HC],rows[:,HC:]],axis=0).astype(bf16)
def unpack(p):
    p=p.astype(f32)
    return jnp.concatenate([p[:24],p[24:]],axis=1)

def send_rows(pc,n,base,slots,dst,ss,rsem,start):
    def one(j,carry):
        t=base+j
        @pl.when(t==pc.me)
        def _():
            if start: pltpu.make_async_copy(slots.at[j],dst,rsem).start()
        @pl.when(t!=pc.me)
        def _():
            d=rcopy(slots.at[j],dst,ss.at[j],rsem,(t//4,t%4))
            if start: d.start()
            else: d.wait_send()
        return carry
    lax.fori_loop(0,n,one,0)

def newton_body(ghalf_ref,stat_ref,left_ref,right_ref,mas_ref,va_ref,vec_ref,sec_ref,
                ln_ref,rn_ref,mn_ref,vg_ref,sn_ref,vn_ref,
                m_ref,x_ref,nb,pb,sb,xb,slots,ggr,uslots,ur,tb,rt,rho,gown_ref, gs,gr,us,ur_sem,es,er):
    pc=Place()
    gown_ref[:,pc.cols]=ghalf_ref[...]
    greet_all(pc)
    b=owned_by(pc)
    owner=pc.xy<3
    nblk=D//RB
    @pl.when(owner)
    def _():
        swap=rcopy(gown_ref.at[:,pc.cols],gown_ref.at[:,pc.cols],es.at[3],er.at[3],pc.sib)
        swap.start()
        swap.wait_recv()
        for c in range(2):
            @pl.when(pc.c==c)
            def _():
                for i in range(nblk):
                    r=slice(i*RB,(i+1)*RB)
                    if c==0: p=dot(gown_ref[r,:],gown_ref[...],1,1)
                    else: p=dot(gown_ref[:,r],gown_ref[...],0,0)
                    x_ref[r,:]=(1-BETA)*p
                    m_ref[r,:]=BETA*stat_ref[r,:]+(1-BETA)*p
        def pk(i,carry):
            slots[i]=pack(x_ref[pl.ds(pl.multiple_of(i*24,8),24),:])
            return carry
        lax.fori_loop(0,32,pk,0)
        send_rows(pc,32,0,slots,ggr.at[2*b+pc.c],gs,gr,True)
        newton(m_ref,x_ref,nb,pb,sb,xb)
        tr=jnp.zeros((1,1),f32)
        for i in range(nblk):
            r=slice(i*RB,(i+1)*RB); tr=tr+diag_sum(x_ref[r,r])
        lam=tr*(1/D)
        for i in range(nblk):
            r=slice(i*RB,(i+1)*RB)
            xb[r,:]=jnp.where(eye_rows(i),x_ref[r,:]-lam,x_ref[r,:]).astype(bf16)
        H=D//2
        send_t=rcopy(tb.at[pl.ds(H,H)],tb.at[pl.ds(H,H)],es.at[0],er.at[0],pc.sib)
        send_r=rcopy(xb,rt,es.at[1],er.at[1],pc.sib)
        send_l=rcopy(rho.at[0],rho.at[1],es.at[2],er.at[2],pc.sib)
        def update(trows,right,lam_r):
            for i in range(2):
                r=pl.ds(trows+i*192,192)
                t=tb[r,:]
                m_ref[pl.ds(i*192,192),:]=lam_r*t.astype(f32)+dot(t,right[...])
        rho[0]=jnp.broadcast_to(lam,(8,128))
        @pl.when(pc.c==0)
        def _():
            for h in (1,0):
                for i in range(2):
                    r=slice(h*H+i*192,h*H+(i+1)*192)
                    tb[r,:]=(lam*gown_ref[r,:].astype(f32)+dot(xb[r,:],gown_ref[...])).astype(bf16)
                if h==1: send_t.start()
            send_r.wait_recv(); send_l.wait_recv()
            update(0,rt,rho[1,0:1,0:1])
            send_t.wait_send()
        @pl.when(pc.c==1)
        def _():
            send_r.start(); send_l.start()
            send_t.wait_recv()
            update(H,xb,lam)
            send_r.wait_send(); send_l.wait_send()
        def pk2(i,carry):
            uslots[i]=pack(m_ref[pl.ds(pl.multiple_of(i*24,8),24),:])
            return carry
        lax.fori_loop(0,16,pk2,0)
        send_rows(pc,16,pc.c*16,uslots,ur.at[b],us,ur_sem,True)
    r=lax.broadcasted_iota(jnp.int32,(D,128),1); j=lax.broadcasted_iota(jnp.int32,(D,128),0)
    pick=jnp.where((j==pc.me*24+r)&(r<24),1.0,0.0).astype(f32)
    vg=lax.dot_general(va_ref[...],pick,(((1,),(0,)),((),())),precision=lax.Precision.HIGHEST,preferred_element_type=f32)[:12,:24]
    sn=BETA_TWO*sec_ref[...]+(1-BETA_TWO)*vg*vg
    vg_ref[...]=vg; sn_ref[...]=sn
    vn_ref[...]=vec_ref[...]-RATE_VEC*vg/(jnp.sqrt(sn)+1e-8)
    pltpu.make_async_copy(ggr,ggr,gr).wait()
    def stats(i,carry):
        ln_ref[i]=BETA*left_ref[i]+unpack(ggr[2*i])
        rn_ref[i]=BETA*right_ref[i]+unpack(ggr[2*i+1])
        return carry
    lax.fori_loop(0,NB,stats,0)
    pltpu.make_async_copy(ur,ur,ur_sem).wait()
    def upd(i,carry):
        mn_ref[i]=mas_ref[i]-RATE*unpack(ur[i])
        return carry
    lax.fori_loop(0,NB,upd,0)
    @pl.when(owner)
    def _():
        rcopy(gown_ref.at[:,pc.cols],gown_ref.at[:,pc.cols],es.at[3],er.at[3],pc.sib).wait_send()
        send_rows(pc,32,0,slots,ggr.at[2*b+pc.c],gs,gr,False)
        send_rows(pc,16,pc.c*16,uslots,ur.at[b],us,ur_sem,False)

def call_newton_step(gown,stat,left,right,mas,va,vec,sec):
    V=pltpu.VMEM; S=jax.ShapeDtypeStruct
    B=pl.BlockSpec(memory_space=V); sem=pltpu.SemaphoreType.DMA
    rows=S((NB,24,D),f32); small=S((NB,24),f32)
    return pl.pallas_call(newton_body,in_specs=[B]*8,out_specs=[B]*6,out_shape=[rows]*3+[small]*3,
        scratch_shapes=[V((D,D),f32)]*2+[V((D,D),bf16)]*4+[V((32,48,HC),bf16),V((24,48,HC),bf16),V((16,48,HC),bf16),V((12,48,HC),bf16),V((D,D),bf16),V((D,D),bf16),V((2,8,128),f32),V((D,D),bf16),
            sem((32,)),sem,sem((16,)),sem,sem((4,)),sem((4,))],
        compiler_params=pltpu.CompilerParams(vmem_limit_bytes=62<<20,collective_id=2,has_side_effects=True))(gown,stat,left,right,mas,va,vec,sec)


def place_params(pg_ref,p_ref):
    r=lax.broadcasted_iota(jnp.int32,(128,D),0); j=lax.broadcasted_iota(jnp.int32,(128,D),1)
    p_ref[...]=jnp.zeros_like(p_ref)
    def chip(m,carry):
        for c in range(2):
            sel=jnp.where((j==(m*2+c)*24+r)&(r<24),1.0,0.0).astype(bf16)
            p_ref[...]+=dot(pg_ref[m//4,m%4,:,c*HC:c*HC+128],sel)
        return carry
    lax.fori_loop(0,16,chip,0)

def keys_of_pair(p,k_ref,ka_ref,v_ref,va_ref,doc_ref):
    cols=pl.ds(pl.multiple_of(p*128,128),128)
    lane=lax.broadcasted_iota(jnp.int32,(256,128),1)
    for t in range(PACK//256):
        rows=pl.ds(t*256,256)
        kp=k_ref[rows,cols].astype(f32); vp=v_ref[rows,cols].astype(f32)
        doc=doc_ref[rows,:]
        for h,lo in enumerate((True,False)):
            off=64 if lo else 0
            k1=onehot_part(kp,lane,lo,doc,1.0,1.0)
            ka_ref[h,rows,:]=jnp.where((lane>=off+8)&(lane<off+11),1.0,k1).astype(bf16)
            va_ref[h,rows,:]=jnp.where((lane<64)==lo,vp,1.0).astype(bf16)

QF=512
def attend_block(p,b,q_ref,ka_ref,va_ref,qa_ref,ctx_ref,doc_ref):
    cols=pl.ds(pl.multiple_of(p*128,128),128)
    rows=pl.ds(pl.multiple_of(b*QF,QF),QF)
    lane=lax.broadcasted_iota(jnp.int32,(QF,128),1)
    low=lane<64
    qp=q_ref[rows,cols].astype(f32)*0.125
    doc=doc_ref[rows,:]
    qf=[onehot_part(qp,lane,lo,doc,0.0,BIG) for lo in (True,False)]
    ss=[dot(qf[h].astype(bf16),ka_ref[h],1,1) for h in range(2)]
    os=[]
    for h,lo in enumerate((True,False)):
        off=64 if lo else 0
        m=jnp.max(ss[h],axis=1,keepdims=True)
        o=dot(jnp.exp(ss[h]-m).astype(bf16),va_ref[h])
        os.append(o)
        q1=qf[h]
        for i,c in enumerate(split3(-(m+jnp.log(o)))): q1=jnp.where(lane==off+8+i,c,q1)
        qa_ref[h,rows,:]=q1.astype(bf16)
    l=pltpu.roll(jnp.where(low,os[1],os[0]),64,1)
    ctx_ref[rows,cols]=(jnp.where(low,os[0],os[1])/l).astype(bf16)

AORDER=(0,1,2,3,4,8,5,9,6,10,7,11)
TT=256
def front_body(len_ref,x_ref,cot_ref,mas_ref,pv_ref,left_ref,right_ref,
               out_o,qa_o,ka_o,v_o,ctx_o,act_o,din_o,dffn_o,hlow_o,dz1_o,dctx_o,wq_o,vec_o,st_ref,
               w_ref,pg_ref,p_ref,sibm,q,k,v,ctx,doc,qa,ka,va,n1,r1,hlow,acc,act,gp,dffn,dctx,out,
               ss,rs,cs,cr,ts,tr,lsem,asem,osem):
    pc=Place()
    greet_all(pc)
    first=rcopy(mas_ref.at[pl.ds(0,3),:,pc.ocols],sibm.at[pl.ds(0,3)],cs.at[0],cr.at[0],pc.sib)
    other=rcopy(mas_ref.at[pl.ds(3,9),:,pc.ocols],sibm.at[pl.ds(3,9)],cs.at[1],cr.at[1],pc.sib)
    first.start(); other.start()
    pg_ref[pc.z,pc.xy,:,pc.cols]=pv_ref[...]
    def assemble(places):
        for pos in places:
            own=mas_ref[AORDER[pos],:,pc.cols]; oth=sibm[AORDER[pos]]
            upper=jnp.where(pc.c==0,own,oth); lower=jnp.where(pc.c==0,oth,own)
            w_ref[pos,pc.z,pc.xy,:,pc.cols]=jnp.concatenate([upper,lower],axis=0).astype(bf16)
    def group(g):
        if isinstance(g,int) and g==0: return Gather(pc,pg_ref,ss.at[0],rs.at[0]).copies()
        return Gather(pc,w_ref.at[g-1],ss.at[g],rs.at[g]).copies()
    NG=13
    def tick(t):
        for s in range(5):
            if isinstance(t,int):
                if 0<=t-s<NG and not (s==0 and t<4): group(t-s).step(s)
            else:
                @pl.when(t-s<NG)
                def _(): group(t-s).step(s)
    def stat(i,start):
        b=(i+pc.me)%NB
        t=owner_of(b)
        for side,ref in enumerate((left_ref,right_ref)):
            mine=(pc.chip==t)&(pc.c==side)
            d=rcopy(ref.at[b],st_ref.at[pc.me],ts.at[b*2+side],tr,(t//2,(t%2)*2+side))
            if start:
                @pl.when(mine)
                def _(): pltpu.make_async_copy(ref.at[b],st_ref.at[pc.me],tr).start()
            @pl.when(jnp.logical_not(mine))
            def _():
                if start: d.start()
                else: d.wait_send()
    copies=[]
    def away(src,dst):
        i=len(copies)
        c=pltpu.make_async_copy(src,dst,lsem.at[i]); c.start(); copies.append(c)
    W=lambda pos: w_ref[pos].reshape(D,D)
    group(0).step(0)
    first.wait_recv()
    for i in range(3):
        assemble([i])
        group(i+1).step(0)
    other.wait_recv()
    assemble(range(3,12))
    for t in range(1,5): tick(t)
    place_params(pg_ref,p_ref)
    t_=lax.broadcasted_iota(jnp.int32,(PACK,128),0)
    end=jnp.int32(0); dd=jnp.zeros((PACK,128),jnp.int32)
    for j in range(8):
        end=end+len_ref[0,j]
        dd=dd+(t_>=end).astype(jnp.int32)
    doc[...]=dd
    for i,(o,b,dst) in enumerate(((q,0,None),(k,None,None),(v,1,v_o))):
        tick(5+i)
        for tl in range(4):
            rows=pl.ds(tl*TT,TT)
            y=dot(x_ref[rows,:],W(i))
            if b is not None: y=y+p_ref[b:b+1,:]
            o[rows,:]=y.astype(bf16)
        if dst is not None: away(o,dst)
        away(w_ref.at[i],wq_o.at[i])
    def pair_copies(p):
        return [pltpu.make_async_copy(s.at[p%2],d.at[p],asem.at[i,p%2]) for i,(s,d) in enumerate(((qa,qa_o),(ka,ka_o)))]
    def slot(n,carry):
        p=n//2; b=n%2
        @pl.when(b==0)
        def _():
            @pl.when(p>=2)
            def _():
                for c in pair_copies(p-2): c.wait()
            keys_of_pair(p,k,ka.at[p%2],v,va,doc)
        attend_block(p,b,q,ka.at[p%2],va,qa.at[p%2],ctx,doc)
        @pl.when(b==1)
        def _():
            for c in pair_copies(p): c.start()
            tick(8+p)
        @pl.when(n%2==1)
        def _(): stat(n//2,True)
        return carry
    lax.fori_loop(0,12,slot,0)
    away(ctx,ctx_o)
    g1,s1,g2,s2=(p_ref[i:i+1,:] for i in (8,9,10,11))
    vec_o[...]=jnp.zeros_like(vec_o)
    def out_proj(tl,carry):
        rows=pl.ds(pl.multiple_of(tl*TT,TT),TT)
        z=x_ref[rows,:].astype(f32)+(dot(ctx[rows,:],W(3))+p_ref[2:3,:])
        n,r=layer_norm(z)
        n1[rows,:]=n
        r1[rows,:]=jnp.broadcast_to(r,(TT,128))
        hlow[rows,:]=(n*g1+s1).astype(bf16)
        return carry
    lax.fori_loop(0,4,out_proj,0)
    tick(14)
    def chunk_copy(c):
        lane=pl.ds(pl.multiple_of(c*D,128),D)
        return pltpu.make_async_copy(act.at[:,lane],act_o.at[:,lane],osem.at[5,c])
    def chunk(c,carry):
        lane=pl.ds(pl.multiple_of(c*D,128),D)
        bias=p_ref[pl.ds(3+c,1),:]
        for tl in range(4):
            rows=pl.ds(tl*TT,TT)
            inner=dot(hlow[rows,:],W(4+2*c))+bias
            a,g=gelu_both(inner)
            al=a.astype(bf16)
            act[rows,lane]=al
            gp[rows,lane]=g.astype(bf16)
            y=dot(al,W(5+2*c))
            @pl.when(c==0)
            def _(): acc[rows,:]=y
            @pl.when(c>0)
            def _(): acc[rows,:]+=y
        chunk_copy(c).start()
        @pl.when(c<2)
        def _(): tick(15+c)
        return carry
    lax.fori_loop(0,4,chunk,0)
    lax.fori_loop(6,NB,lambda b,c: (stat(b,True),c)[1],0)
    away(hlow,hlow_o)
    pltpu.make_async_copy(cot_ref,out,lsem.at[20]).start()
    pltpu.make_async_copy(cot_ref,out,lsem.at[20]).wait()
    def tile_copies(tl):
        rows=pl.ds(pl.multiple_of(tl*TT,TT),TT)
        return [pltpu.make_async_copy(s.at[rows],d.at[rows],osem.at[i,tl]) for i,(s,d) in enumerate(((out,out_o),(gp,din_o),(dffn,dffn_o),(acc,dz1_o),(dctx,dctx_o)))]
    def tile(tl,carry):
        rows=pl.ds(pl.multiple_of(tl*TT,TT),TT)
        n1t=n1[rows,:]
        z=(n1t*g1+s1)+(acc[rows,:]+p_ref[7:8,:])
        n2,r2=layer_norm(z)
        e=out[rows,:].astype(f32)
        out[rows,:]=(n2*g2+s2).astype(bf16)
        c2=e*g2
        dz2=r2*(c2-jnp.mean(c2,axis=-1,keepdims=True)-n2*jnp.mean(c2*n2,axis=-1,keepdims=True))
        df=dz2.astype(bf16)
        dffn[rows,:]=df
        vec_o[10:11,:]+=jnp.sum(e*n2,axis=0,keepdims=True)
        vec_o[11:12,:]+=jnp.sum(e,axis=0,keepdims=True)
        vec_o[7:8,:]+=jnp.sum(df.astype(f32),axis=0,keepdims=True)
        dh=dz2
        for c in range(4):
            lane=pl.ds(c*D,D)
            dact=dot(df,W(5+2*c),1,1)
            din=(dact*gp[rows,lane].astype(f32)).astype(bf16)
            gp[rows,lane]=din
            vec_o[3+c:4+c,:]+=jnp.sum(din.astype(f32),axis=0,keepdims=True)
            dh=dh+dot(din,W(4+2*c),1,1)
        vec_o[8:9,:]+=jnp.sum(dh*n1t,axis=0,keepdims=True)
        vec_o[9:10,:]+=jnp.sum(dh,axis=0,keepdims=True)
        c1=dh*g1
        dz1=r1[rows,0:1]*(c1-jnp.mean(c1,axis=-1,keepdims=True)-n1t*jnp.mean(c1*n1t,axis=-1,keepdims=True))
        acc[rows,:]=dz1
        dat=dz1.astype(bf16)
        vec_o[2:3,:]+=jnp.sum(dat.astype(f32),axis=0,keepdims=True)
        dctx[rows,:]=dot(dat,W(3),1,1).astype(bf16)
        for c in tile_copies(tl): c.start()
        return carry
    lax.fori_loop(0,4,tile,0)
    for c in copies: c.wait()
    for p in (4,5):
        for c in pair_copies(p): c.wait()
    for i in range(4):
        chunk_copy(i).wait()
        for c in tile_copies(i): c.wait()
    first.wait_send(); other.wait_send()
    group(0).done()
    lax.fori_loop(1,NG,lambda g,c: (group(g).done(),c)[1],0)
    lax.fori_loop(0,NB,lambda b,c: (stat(b,False),c)[1],0)
    @pl.when(pc.xy<3)
    def _(): pltpu.make_async_copy(st_ref,st_ref,tr).wait()

def call_front(lengths,x,cot,masters,pv,left,right):
    V=pltpu.VMEM; S=jax.ShapeDtypeStruct; A=pl.ANY
    B=lambda m: pl.BlockSpec(memory_space=m)
    sem=pltpu.SemaphoreType.DMA
    T=lambda w,d: S((PACK,w),d)
    return pl.pallas_call(front_body,
        in_specs=[B(pltpu.SMEM),B(V),B(A),B(V),B(V),B(A),B(A)],
        out_specs=[B(A)]*12+[B(V),B(A)],
        out_shape=[T(D,bf16)]+[S((6,2,PACK,128),bf16)]*2+[T(D,bf16)]*2+[T(FF,bf16),T(FF,bf16),T(D,bf16),T(D,bf16),T(D,f32),T(D,bf16),S((3,4,4,MR,D),bf16),S((16,D),f32),S((32,24,D),f32)],
        scratch_shapes=[V((NB,4,4,MR,D),bf16),V((4,4,16,D),bf16),V((16,D),f32),V((NB,24,HC),f32)]+[V((PACK,D),bf16)]*4+
            [V((PACK,128),jnp.int32),V((2,2,PACK,128),bf16),V((2,2,PACK,128),bf16),V((2,PACK,128),bf16),V((PACK,D),f32),V((PACK,128),f32),V((PACK,D),bf16),V((PACK,D),f32),
             V((PACK,FF),bf16),V((PACK,FF),bf16),V((PACK,D),bf16),V((PACK,D),bf16),V((PACK,D),bf16),
             sem((13,11)),sem((13,11)),sem((2,)),sem((2,)),sem((24,)),sem,sem((24,)),sem((2,2)),sem((6,4))],
        compiler_params=pltpu.CompilerParams(vmem_limit_bytes=63<<20,collective_id=0,has_side_effects=True))(lengths,x,cot,masters,pv,left,right)


NGR=12
def sum_scratch():
    V=pltpu.VMEM; nb=NGR
    return dict(rc=V((nb,4,4,MR,HC),bf16),xa=V((nb,2,2,MR,HC),bf16),yb=V((nb,2,2,MR,HC),bf16),
        s2a=V((nb,2,MR,HC),bf16),s2b=V((nb,2,MR,HC),bf16),ya=V((nb,2,MR,HC),bf16),xb=V((nb,2,MR,HC),bf16),
        s3=V((nb,4,MR,HC),bf16),zr=V((nb,3,MR,HC),bf16),fin=V((nb,MR,HC),f32),finb=V((nb,MR,HC),bf16),hr=V((nb,24,HC),f32))
SKEYS=list(sum_scratch())

class GroupSum:
    def __init__(self,pc,g_ref,R,out_ref,gown_ref,ss,rs,os_,orr):
        self.pc,self.gr,self.RR,self.out,self.gown=pc,g_ref,R,out_ref,gown_ref
        self.ss,self.rs,self.os_,self.orr=ss,rs,os_,orr
    def mk(self,g,i,src,dst,dev): return rcopy(src,dst,self.ss.at[g,i],self.rs.at[g,i],dev)
    def of(self,g): return self.gr.at[g],{k:v.at[g] for k,v in self.RR.items()}
    def core(self,g):
        G,R=self.of(g); return self.mk(g,0,G.at[:,:,:,self.pc.ocols],R["rc"],self.pc.sib)
    def xa(self,g):
        G,R=self.of(g); pc=self.pc; return self.mk(g,1,G.at[pl.ds(0,2),pl.ds((1-pc.x)*2,2),:,pc.cols],R["xa"],pc.xn)
    def yb(self,g,i):
        G,R=self.of(g); pc=self.pc; return self.mk(g,2+i,G.at[pl.ds(2,2),i*2+1-pc.y,:,pc.cols],R["yb"].at[i],pc.yn)
    def ya(self,g):
        G,R=self.of(g); return self.mk(g,4,R["s2a"],R["ya"],self.pc.yn)
    def xb(self,g):
        G,R=self.of(g); return self.mk(g,5,R["s2b"],R["xb"],self.pc.xn)
    def zz(self,g,k):
        G,R=self.of(g); pc=self.pc; return self.mk(g,5+k,R["s3"].at[(pc.z+k)%NZ],R["zr"].at[k-1],pc.zpeer(k))
    def home(self,g):
        G,R=self.of(g); pc=self.pc; return self.mk(g,9,R["fin"].at[pl.ds(pl.multiple_of((1-pc.c)*24,8),24)],R["hr"],pc.sib)
    def step0(self,g): self.core(g).start()
    def step1(self,g):
        pc=self.pc; G,R=self.of(g)
        self.core(g).wait_recv()
        for z in range(4):
            G[z,:,:,pc.cols]=(G[z,:,:,pc.cols].astype(f32)+R["rc"][z].astype(f32)).astype(bf16)
        self.xa(g).start()
        for i in range(2): self.yb(g,i).start()
    def step2(self,g):
        pc=self.pc; G,R=self.of(g)
        self.xa(g).wait_recv()
        R["s2a"][...]=(G[0:2,pc.x*2+1-pc.y,:,pc.cols].astype(f32)+R["xa"][:,1-pc.y].astype(f32)).astype(bf16)
        self.ya(g).start()
        for i in range(2): self.yb(g,i).wait_recv()
        R["s2b"][...]=(G[2:4,(1-pc.x)*2+pc.y,:,pc.cols].astype(f32)+R["yb"][1-pc.x].astype(f32)).astype(bf16)
        self.xb(g).start()
    def step3(self,g):
        pc=self.pc; G,R=self.of(g)
        self.ya(g).wait_recv(); self.xb(g).wait_recv()
        a=G[0:2,pc.xy,:,pc.cols].astype(f32)+R["xa"][:,pc.y].astype(f32)+R["ya"][...].astype(f32)
        b=G[2:4,pc.xy,:,pc.cols].astype(f32)+R["yb"][pc.x].astype(f32)+R["xb"][...].astype(f32)
        R["s3"][0:2]=a.astype(bf16); R["s3"][2:4]=b.astype(bf16)
        ab=jnp.where(pc.z%2==0,jnp.stack([a[0],b[0]]),jnp.stack([a[1],b[1]]))
        R["fin"][...]=jnp.where(pc.z<2,ab[0],ab[1])
        for k in (1,2,3): self.zz(g,k).start()
    def targets(self,g,act):
        pc=self.pc; G,R=self.of(g)
        def whole(b):
            act(R["finb"],self.gown.at[pc.chip],0,owner_of(b))
        def slab(j):
            for i in range(3):
                act(R["finb"].at[:,pl.ds(i*128,128)],self.gown.at[pc.chip,:,pl.ds(pl.multiple_of(j*128,128),128)],i,owner_of(i))
        if isinstance(g,int):
            if g<9: whole(8+g//2-4*(g%2)-9*(g//8))
            else: slab(g-9)
        else:
            @pl.when(g<9)
            def _(): whole(8+g//2-4*(g%2)-9*(g//8))
            @pl.when(g>=9)
            def _(): slab(g-9)
    def step4(self,g):
        pc=self.pc; G,R=self.of(g)
        for k in (1,2,3): self.zz(g,k).wait_recv()
        s=R["fin"][...]
        for k in range(3): s=s+R["zr"][k].astype(f32)
        R["fin"][...]=s
        R["finb"][...]=s.astype(bf16)
        self.home(g).start()
        def send(src,dst,i,t):
            mine=pc.chip==t
            @pl.when(mine)
            def _(): pltpu.make_async_copy(src,dst,self.orr).start()
            @pl.when(jnp.logical_not(mine))
            def _(): rcopy(src,dst,self.os_.at[g,i],self.orr,(t//2,(t%2)*2+pc.c)).start()
        self.targets(g,send)
    def step5(self,g):
        pc=self.pc; G,R=self.of(g)
        self.home(g).wait_recv()
        def whole(b):
            self.out[b,:,pc.cols]=R["fin"][pl.ds(pl.multiple_of(pc.c*24,8),24)]
            self.out[b,:,pc.ocols]=R["hr"][...]
        def slab(j):
            for i in range(3):
                self.out[i,:,pl.ds(pl.multiple_of((pc.c*3+j)*128,128),128)]=R["fin"][pl.ds(pl.multiple_of(pc.c*24,8),24),i*128:(i+1)*128]
                self.out[i,:,pl.ds(pl.multiple_of(((1-pc.c)*3+j)*128,128),128)]=R["hr"][:,i*128:(i+1)*128]
        if isinstance(g,int):
            if g<9: whole(8+g//2-4*(g%2)-9*(g//8))
            else: slab(g-9)
        else:
            @pl.when(g<9)
            def _(): whole(8+g//2-4*(g%2)-9*(g//8))
            @pl.when(g>=9)
            def _(): slab(g-9)
    def done(self,g):
        pc=self.pc
        for d in (self.core,self.xa,self.ya,self.xb,self.home): d(g).wait_send()
        for i in range(2): self.yb(g,i).wait_send()
        for k in (1,2,3): self.zz(g,k).wait_send()
        def wait(src,dst,i,t):
            @pl.when(pc.chip!=t)
            def _(): rcopy(src,dst,self.os_.at[g,i],self.orr,(t//2,(t%2)*2+pc.c)).wait_send()
        self.targets(g,wait)

KB_=512
def prepare_pair(p,v,ctx,do,doa,va):
    cols=pl.ds(pl.multiple_of(p*128,128),128)
    lane=lax.broadcasted_iota(jnp.int32,(256,128),1)
    i=lax.broadcasted_iota(jnp.int32,(128,128),0); j=lax.broadcasted_iota(jnp.int32,(128,128),1)
    cross=jnp.where((i<64)!=(j<64),-1.0,0.0).astype(bf16)
    for t in range(PACK//256):
        rows=pl.ds(t*256,256)
        vp=v[rows,cols].astype(f32)
        dop=do[rows,cols].astype(f32); prod=dop*ctx[rows,cols].astype(f32)
        dd=sum(dot(c.astype(bf16),cross) for c in split3(prod))
        parts=split3(dd)
        for h,lo in enumerate((True,False)):
            keep=(lane<64)==lo
            off=64 if lo else 0
            d1=jnp.where(keep,dop,0.0)
            for n,c in enumerate(parts): d1=jnp.where(lane==off+n,c,d1)
            doa[h,rows,:]=d1.astype(bf16)
            v1=jnp.where(keep,vp,0.0)
            va[h,rows,:]=jnp.where((lane>=off)&(lane<off+3),1.0,v1).astype(bf16)

def back_block(p,b,dk_ref,dv_ref,qa,doa,ka,va,dqa):
    cols=pl.ds(pl.multiple_of(p*128,128),128)
    rows=pl.ds(pl.multiple_of(b*KB_,KB_),KB_)
    low=lax.broadcasted_iota(jnp.int32,(KB_,128),1)<64
    lowq=lax.broadcasted_iota(jnp.int32,(PACK,128),1)<64
    r=[]
    for h in range(2):
        kh=ka[h,rows,:]
        pr=jnp.exp(dot(kh,qa[h],1,1))
        dp=dot(va[h,rows,:],doa[h],1,1)
        ds=(pr*dp).astype(bf16)
        r.append((dot(pr.astype(bf16),doa[h]),dot(ds,qa[h]),dot(ds,kh,0,0)))
    dq=jnp.where(lowq,r[0][2],r[1][2])
    @pl.when(b==0)
    def _(): dqa[...]=dq
    @pl.when(b>0)
    def _(): dqa[...]+=dq
    dv_ref[rows,cols]=jnp.where(low,r[0][0],r[1][0]).astype(bf16)
    dk_ref[rows,cols]=jnp.where(low,r[0][1],r[1][1]).astype(bf16)

def back_body(x_ref,qa_i,ka_i,v_i,ctx_i,do_i,act_i,din_i,dffn_i,hlow_i,dz1_i,wq_i,vec_ref,
              ig_o,out_ref,vout_ref,gown_ref,*rest):
    R=dict(zip(SKEYS,rest[:len(SKEYS)]))
    (g_ref,ctx,w_last,act,din,dffn,hlow,acc,qa,doa,ka,va,dqa,vcur,vbuf,
     ss,rs,os_,orr,vs,vr,lsem,asem)=rest[len(SKEYS):]
    pc=Place()
    loads={}
    def load(name,src,dst):
        c=pltpu.make_async_copy(src,dst,lsem.at[len(loads)]); c.start(); loads[name]=c
    half=lambda ref,c: ref.at[:,pl.ds(c*D,D)]
    load("act0",half(act_i,0),act.at[0]); load("dffn",dffn_i,dffn)
    load("hlow",hlow_i,hlow); load("din0",half(din_i,0),din.at[0])
    load("act1",half(act_i,1),act.at[1]); load("din1",half(din_i,1),din.at[1])
    for n,s,d in (("acc",dz1_i,acc),("ctx",ctx_i,ctx)): load(n,s,d)
    q,v,do,k=act.at[0],din.at[0],dffn,act.at[1]
    late={5:("v",v_i,v),7:("do",do_i,do)}
    def pair_loads(pi):
        p=3*(pi%2)+pi//2
        return [pltpu.make_async_copy(s.at[p],d.at[pi%2],asem.at[i,pi%2]) for i,(s,d) in enumerate(((qa_i,qa),(ka_i,ka)))]
    for c in pair_loads(0): c.start()
    greet_all(pc)
    gs=GroupSum(pc,g_ref,R,out_ref,gown_ref,ss,rs,os_,orr)
    vsum=VecSum(pc,vcur,vbuf,vs,vr)
    def product(g,a,b):
        for r in range(4):
            g_ref[g,r]=dot(a[:,r*192:(r+1)*192],b,0,0).astype(bf16).reshape(4,MR,D)
    loads["dffn"].wait()
    for i in range(9):
        c=i//2
        if i==8:
            loads["ctx"].wait(); loads["acc"].wait()
            product(i,ctx,acc[...].astype(bf16))
        elif i%2==0:
            loads[f"act{c}"].wait()
            product(i,act.at[c%2],dffn[...])
            if c<2: load(f"act{c+2}",half(act_i,c+2),act.at[c%2])
        else:
            if c==0: loads["hlow"].wait()
            loads[f"din{c}"].wait()
            product(i,hlow,din[c%2])
            if c<2: load(f"din{c+2}",half(din_i,c+2),din.at[c%2])
        if i in late: load(*late[i])
        gs.step0(i)
        if i>=1: gs.step1(i-1)
    gs.step2(0)
    wrow=pl.ds(0,D)
    wdst=[din.at[1,wrow],hlow.at[wrow],w_last]
    for i in range(3): load(f"w{i}",wq_i.at[i],wdst[i])
    for n in ("v","do"): loads[n].wait()
    def slot(n,carry):
        pi=n//2; b=n%2; j=pi//2; cc=pi%2; p=3*cc+j; side=pi%2
        cols=pl.ds(pl.multiple_of(p*128,128),128)
        @pl.when(b==0)
        def _():
            for c in pair_loads(pi): c.wait()
            @pl.when(pi<5)
            def _():
                for c in pair_loads(pi+1): c.start()
            prepare_pair(p,v,ctx,do,doa,va)
        back_block(p,b,k,v,qa.at[side],doa,ka.at[side],va,dqa)
        @pl.when(b==1)
        def _():
            q[:,cols]=(dqa[...]*0.125).astype(bf16)
            al=jnp.concatenate([q[:,cols],k[:,cols],v[:,cols]],axis=1)
            lane=pl.ds(pl.multiple_of(cc*HC,128),HC)
            for r in range(4):
                g_ref[9+j,r,:,:,lane]=dot(x_ref[:,r*192:(r+1)*192],al,0,0).astype(bf16).reshape(4,MR,HC)
            vcur[0,0:1,cols]=jnp.sum(q[:,cols].astype(f32),axis=0,keepdims=True)
            vcur[0,1:2,cols]=jnp.sum(v[:,cols].astype(f32),axis=0,keepdims=True)
        @pl.when(n==0)
        def _(): gs.step1(8)
        @pl.when(n<=9)
        def _(): gs.step2(1+n)
        @pl.when(n<=10)
        def _(): gs.step3(n)
        @pl.when(n>=1)
        def _(): gs.step4(n-1)
        @pl.when(n>=2)
        def _(): gs.step5(n-2)
        @pl.when((n==4)|(n==8))
        def _(): gs.step1(8+n//4)
        @pl.when((n==3)|(n==7))
        def _(): gs.step0(9+n//7)
        return carry
    vcur[0]=vec_ref[...]
    lax.fori_loop(0,12,slot,0)
    gs.step0(11)
    vsum.step(0)
    for i in range(3): loads[f"w{i}"].wait()
    def grad_tile(t):
        rows=pl.ds(t*256,256)
        a=acc[rows,:]
        for d,w in zip((q,k,v),wdst): a=a+dot(d[rows,:],w[...],1,1)
        acc[rows,:]=a
    grad_tile(0);
    gs.step5(10); gs.step1(11); vsum.step(1)
    grad_tile(1); grad_tile(2); vsum.step(2)
    gs.step2(11); grad_tile(3); vsum.step(3)
    away=pltpu.make_async_copy(acc,ig_o,lsem.at[31]); away.start()
    gs.step3(11); vsum.step(4)
    gs.step4(11); vsum.step(5)
    gs.step5(11)
    vout_ref[...]=vcur[5]
    vsum.done()
    lax.fori_loop(0,NGR,lambda g,c: (gs.done(g),c)[1],0)
    away.wait()
    @pl.when(pc.xy<3)
    def _(): pltpu.make_async_copy(gown_ref,gown_ref,orr).wait()

def call_back(x,qa,ka,v,ctx,dctx,act,din,dffn,hlow,dz1,wq,vec):
    V=pltpu.VMEM; S=jax.ShapeDtypeStruct; A=pl.ANY
    B=lambda m: pl.BlockSpec(memory_space=m)
    sem=pltpu.SemaphoreType.DMA
    T=V((PACK,D),bf16); H=V((2,PACK,128),bf16)
    return pl.pallas_call(back_body,
        in_specs=[B(V)]+[B(A)]*11+[B(V)],
        out_specs=[B(A),B(V),B(V),B(A)],
        out_shape=[S((PACK,D),f32),S((NB,24,D),f32),S((16,D),f32),S((16,MR,HC),bf16)],
        scratch_shapes=list(sum_scratch().values())+[V((NGR,4,4,MR,D),bf16),T,V((D,D),bf16)]+[V((2,PACK,D),bf16),V((2,PACK,D),bf16),T,T,V((PACK,D),f32)]+[V((2,2,PACK,128),bf16),H,V((2,2,PACK,128),bf16),H]+
            [V((PACK,128),f32),V((6,16,D),f32),V((5,16,D),f32),sem((NGR,10)),sem((NGR,10)),sem((NGR,3)),sem,sem((5,)),sem((5,)),sem((32,)),sem((2,2))],
        compiler_params=pltpu.CompilerParams(vmem_limit_bytes=63<<20,collective_id=1,has_side_effects=True))(x,qa,ka,v,ctx,dctx,act,din,dffn,hlow,dz1,wq,vec)


def gather_rows(a):
    return lax.all_gather(a,("dp","head"),axis=1,tiled=True)

def doc_lengths(lengths):
    return lax.dynamic_slice_in_dim(lengths,lax.axis_index("head"),1,axis=0)

def layer(tokens,cotangent,lengths,w,params):
    q,k,v,ctx,lse,n1,r1=call_a(lengths,tokens,w,params)
    out,dz1,dctx,dwo,dw1,dw2,vec=call_b(cotangent,n1,r1,ctx,w,params)
    ig,dwqkv,vq=call_c(lengths,tokens,q,k,v,ctx,dctx,lse,dz1,w)
    terms=jnp.concatenate([dwqkv,dwo[None],dw1,dw2],axis=0)
    vec=jnp.concatenate([vq[0:1],vq[2:3],vec[2:]],axis=0)
    return out,ig,terms,vec

def on_slice(tokens,cotangent,lengths,masters,vectors,left,right,second):
    pv=jnp.pad(vectors,((0,4),(0,HC-24))).astype(bf16)
    lens=doc_lengths(lengths)
    out,qa,ka,v,ctx,act,din,dffn,hlow,dz1,dctx,wq,vec,stat=call_front(lens,tokens,cotangent,masters,pv,left,right)
    ig,grads,vec_all,gown=call_back(tokens,qa,ka,v,ctx,dctx,act,din,dffn,hlow,dz1,wq.reshape(3,D,D),vec)
    ln,rn,mn,vg,sn,vn=call_newton_step(gown.reshape(D,HC),stat.reshape(D,D),left,right,masters,vec_all,vectors,second)
    return out,ig,grads,ln,rn,mn,vg,sn,vn

def on_any(tokens,cotangent,lengths,masters,vectors,left,right,second):
    axes=("dp","head")
    me=lax.axis_index("dp")*lax.axis_size("head")+lax.axis_index("head")
    share=masters.shape[1]
    w=gather_rows(masters.astype(bf16))
    params=gather_rows(vectors.astype(bf16)).astype(f32)
    out,ig,terms,vec=layer(tokens,cotangent,doc_lengths(lengths),w,params)
    grads=lax.psum_scatter(terms.astype(f32),axes,scatter_dimension=1,tiled=True)
    vg=lax.psum_scatter(vec[:12],axes,scatter_dimension=1,tiled=True)
    low=grads.astype(bf16)
    g=gather_rows(low)
    ein=partial(jnp.einsum,preferred_element_type=f32)
    cols=lax.dynamic_slice_in_dim(g,me*share,share,axis=2)
    ln=BETA*left+(1-BETA)*ein("kid,kjd->kij",low,g)
    rn=BETA*right+(1-BETA)*ein("kdi,kdj->kij",cols,g)
    item=jnp.minimum(me,2*NB-1)
    own=lax.dynamic_index_in_dim(jnp.concatenate([gather_rows(ln),gather_rows(rn)],axis=0),item,0,keepdims=False)
    root=call_newton(own)
    place=jnp.where((jnp.arange(2*NB)==me)[:,None,None],root[None],0.0)
    rows=lax.psum_scatter(place,axes,scatter_dimension=1,tiled=True)
    rr=gather_rows(rows[NB:])
    hi=partial(jnp.einsum,"kij,kjl->kil",precision=lax.Precision.HIGHEST)
    mn=masters-RATE*hi(hi(rows[:NB],g.astype(f32)),rr)
    sn=BETA_TWO*second+(1-BETA_TWO)*vg*vg
    vn=vectors-RATE_VEC*vg/(jnp.sqrt(sn)+1e-8)
    return out,ig,grads,ln,rn,mn,vg,sn,vn

def solution(mesh):
    rows=P(("dp","head"),None); blocks=P(None,("dp","head"),None); vecs=P(None,("dp","head"))
    on_device=on_slice if dict(mesh.shape)=={"dp":8,"head":4} else on_any
    return jax.shard_map(on_device,mesh=mesh,
        in_specs=(rows,rows,P("dp",None),blocks,vecs,blocks,blocks,vecs),
        out_specs=(rows,rows,blocks,blocks,blocks,blocks,vecs,vecs,vecs),check_vma=False)
```

profile of v0, /device:TPU:11, one launch (start us, length us, event | category | flops | bytes accessed | tf_op | source)
XLA Modules:
  0.0 339.2 jit_solution(12122611875924040688)
XLA Ops:
  0.6 0.0 copy-start
  0.7 0.7 copy-done
  1.3 0.5 constant_dynamic-slice_fusion.len_ref
  1.8 0.7 convert.4
  2.5 0.6 pad.5.pv_ref
  3.2 140.0 %shard_map.151 = (bf16[1024,768]{1,0:T(8,128)(2,1)}, bf16[6,2,1024,128]{3,2,1,0:T(8,128)(2,1)}, bf16[6,2,1024,128]{3,2,1,0:T(8,128)(2,1)}, bf16[1024,768]{1,0:T(...) custom-call(s32[1,8]{1,0:T(1,128)} %constant_dynamic-slice_fusion.le, ...), custom_call_target="tpu_custom_call" | custom-call | tf_op jit(solution)/shard_map/pallas_call | solution.py:941
  143.2 121.4 %shard_map.152 = (f32[1024,768]{1,0:T(8,128)}, f32[12,24,768]{2,1,0:T(8,128)}, f32[16,768]{1,0:T(8,128)}, bf16[16,48,384]{2,1,0:T(8,128)(2,1)}) custom-call(bf16[1024,768]{1,0:T(8,128)(2,1)} %x_ref.3, bf16[6,2,1024,128]{3,2,1,0:T(8,128)(2,1)} %get-tuple-element.34.qa_i, bf16[6,2,1024,128]{3,2,1,0:T(8,128)(2,1)} %get-tuple-element.35.ka_i, ...), custom_call_target="tpu_custom_call" | custom-call | tf_op jit(solution)/shard_map/pallas_call | solution.py:1218
  264.6 0.0 copy-start.2
  264.6 64.7 %shard_map.153 = (f32[12,24,768]{2,1,0:T(8,128)}, f32[12,24,768]{2,1,0:T(8,128)}, f32[12,24,768]{2,1,0:T(8,128)}, f32[12,24]{1,0:T(8,128)}, f32[12,24]{1,0:T(8,128)}, /*index=5*/f32[12,24]{1,0:T(8,128)}) custom-call(bf16[768,384]{1,0:T(8,128)(2,1)} %bitcast.5, f32[768,768]{1,0:T(8,128)} %bitcast.4, f32[12,24,768]{2,1,0:T(8,128)} %left_ref.3, ...), custom_call_target="tpu_custom_call" | custom-call | tf_op jit(solution)/shard_map/pallas_call | solution.py:707
  329.3 0.0 copy-start.1
  329.3 0.0 copy-done.2
  329.3 1.1 copy.26
  330.4 1.3 copy-done.1
  331.7 1.7 copy.27
  333.4 0.1 copy-done.3
  333.5 0.9 copy.28
  334.4 0.0 copy-done.6
  334.4 0.9 copy.29
  335.4 0.0 copy-done.5
  335.4 0.9 copy.30
  336.3 0.9 copy.31
  337.2 0.6 copy.32
  337.8 0.6 copy.33
  338.4 0.6 copy.34
  (11 shorter events, 0.0 us)
Async XLA Ops:
  0.6 0.7 copy-start
  264.6 64.7 %copy-start.2 = (bf16[1024,768]{1,0:T(8,128)(2,1)S(1)}, bf16[1024,768]{1,0:T(8,128)(2,1)}, u32[]{:S(2)}) copy-start(bf16[1024,768]{1,0:T(8,128)(2,1)} %get-tuple-element.66) | copy-start | bytes 4718596
  329.3 2.5 copy-start.1
  331.7 1.8 copy-start.3
  331.7 2.7 copy-start.6
  333.5 1.8 copy-start.5
  333.5 2.8 copy-start.4
  334.4 2.8 copy-start.9
  334.4 3.4 copy-start.8
  334.4 4.0 %copy-start.7 = (f32[12,24]{1,0:T(8,128)S(1)}, f32[12,24]{1,0:T(8,128)}, u32[]{:S(2)}) copy-start(f32[12,24]{1,0:T(8,128)} %get-tuple-element.74) | copy-start | bytes 3460
where the time goes:
time: 345 us; the launch traced here: 339 us
  Pallas kernels  326 us (94%)
  local copies, waits for them, and re-layouts  11.5 us (3%)
    pallas_call x1, Pallas kernels, call_front(): pl.pallas_call(front_body, in_specs=[B(pltpu.SMEM), B(V), B(A), B(V), B(V...  140 us
    pallas_call x1, Pallas kernels, call_back(): pl.pallas_call(back_body, in_specs=[B(V)] + [B(A)] * 11 + [B(V)], out_spe...  121 us
    pallas_call x1, Pallas kernels, call_newton_step(): pl.pallas_call(newton_body, in_specs=[B] * 8, out_specs=[B] * 6, out_shap...  64.7 us
    unnamed x29, local copies, waits for them, and re-layouts  10.4 us

commit v1 on v0

--- a/solution.py
+++ b/solution.py
@@ -246,7 +246,7 @@
 def eye_rows(rb):
     i=lax.broadcasted_iota(jnp.int32,(RB,D),0)+rb*RB; j=lax.broadcasted_iota(jnp.int32,(RB,D),1)
     return i==j
-def newton(m_ref,x_ref,nb_ref,pb_ref,sb_ref,xb_ref):
+def newton(m_ref,x_ref,nb_ref,pb_ref,sb_ref,xb_ref,between=lambda k: None):
     nblk=D//RB
     R=[slice(i*RB,(i+1)*RB) for i in range(nblk)]
     tot=jnp.zeros((1,1),f32); tr=jnp.zeros((1,1),f32)
@@ -292,7 +292,11 @@
                 al2=al2+diag_sum(m[:,R[i]])
         return al2*(1/D),be2*(1/D)
     al,be=iteration(0,al,None,first=True)
-    al,be=lax.fori_loop(1,7,lambda k,ab:iteration(k,*ab),(al,be))
+    def step(k,ab):
+        ab=iteration(k,*ab)
+        between(k)
+        return ab
+    al,be=lax.fori_loop(1,7,step,(al,be))
     iteration(7,al,be,last=True)
     for i in range(nblk):
         x_ref[R[i],:]=x_ref[R[i],:]*s
@@ -596,6 +600,12 @@
     p=p.astype(f32)
     return jnp.concatenate([p[:24],p[24:]],axis=1)
 
+def send_row(pc,t,src,dst,ssem,rsem):
+    @pl.when(t==pc.me)
+    def _(): pltpu.make_async_copy(src,dst,rsem).start()
+    @pl.when(t!=pc.me)
+    def _(): rcopy(src,dst,ssem,rsem,(t//4,t%4)).start()
+
 def send_rows(pc,n,base,slots,dst,ss,rsem,start):
     def one(j,carry):
         t=base+j
@@ -610,35 +620,57 @@
         return carry
     lax.fori_loop(0,n,one,0)
 
-def newton_body(ghalf_ref,stat_ref,left_ref,right_ref,mas_ref,va_ref,vec_ref,sec_ref,
+def newton_body(ghalf_ref,statl_ref,statr_ref,left_ref,right_ref,mas_ref,va_ref,vec_ref,sec_ref,
                 ln_ref,rn_ref,mn_ref,vg_ref,sn_ref,vn_ref,
-                m_ref,x_ref,nb,pb,sb,xb,slots,ggr,uslots,ur,tb,rt,rho,gown_ref, gs,gr,us,ur_sem,es,er):
+                m_ref,x_ref,nb,pb,sb,xb,slots,ggr,uslots,ur,tb,rt,rho,gown_ref,vcur,vbuf,gg, gs,gr,us,ur_sem,es,er,vs,vr):
     pc=Place()
     gown_ref[:,pc.cols]=ghalf_ref[...]
+    vcur[0]=va_ref[...]
     greet_all(pc)
+    vsum=VecSum(pc,vcur,vbuf,vs,vr)
+    vsum.step(0)
     b=owned_by(pc)
     owner=pc.xy<3
     nblk=D//RB
+    swap=lambda: rcopy(gown_ref.at[:,pc.cols],gown_ref.at[:,pc.cols],es.at[3],er.at[3],pc.sib)
+    @pl.when(owner)
+    def _(): swap().start()
+    vsum.step(1)
     @pl.when(owner)
     def _():
-        swap=rcopy(gown_ref.at[:,pc.cols],gown_ref.at[:,pc.cols],es.at[3],er.at[3],pc.sib)
-        swap.start()
-        swap.wait_recv()
-        for c in range(2):
-            @pl.when(pc.c==c)
-            def _():
-                for i in range(nblk):
-                    r=slice(i*RB,(i+1)*RB)
-                    if c==0: p=dot(gown_ref[r,:],gown_ref[...],1,1)
-                    else: p=dot(gown_ref[:,r],gown_ref[...],0,0)
-                    x_ref[r,:]=(1-BETA)*p
-                    m_ref[r,:]=BETA*stat_ref[r,:]+(1-BETA)*p
-        def pk(i,carry):
-            slots[i]=pack(x_ref[pl.ds(pl.multiple_of(i*24,8),24),:])
-            return carry
-        lax.fori_loop(0,32,pk,0)
-        send_rows(pc,32,0,slots,ggr.at[2*b+pc.c],gs,gr,True)
-        newton(m_ref,x_ref,nb,pb,sb,xb)
+        @pl.when(pc.c==0)
+        def _():
+            for i in range(nblk):
+                r=slice(i*RB,(i+1)*RB)
+                gg[r,:]=(1-BETA)*dot(ghalf_ref[r,:],ghalf_ref[...],1,1)
+            swap().wait_recv()
+            for i in range(nblk):
+                r=slice(i*RB,(i+1)*RB)
+                p=gg[r,:]+(1-BETA)*dot(gown_ref[r,HC:],gown_ref[:,HC:],1,1)
+                gg[r,:]=p
+                m_ref[r,:]=BETA*statl_ref[r,:]+p
+        @pl.when(pc.c==1)
+        def _():
+            swap().wait_recv()
+            for i in range(nblk):
+                r=slice(i*RB,(i+1)*RB)
+                p=(1-BETA)*dot(gown_ref[:,r],gown_ref[...],0,0)
+                gg[r,:]=p
+                m_ref[r,:]=BETA*statr_ref[r,:]+p
+        def between(k):
+            def piece(t,carry):
+                slots[t]=pack(gg[pl.ds(pl.multiple_of(t*24,8),24),:])
+                send_row(pc,t,slots.at[t],ggr.at[2*b+pc.c],gs.at[t],gr)
+                return carry
+            @pl.when(k<3)
+            def _(): lax.fori_loop((k-1)*16,k*16,piece,0)
+            @pl.when(k==2)
+            def _(): vsum.step(2)
+            @pl.when(k==4)
+            def _(): vsum.step(3)
+            @pl.when(k==6)
+            def _(): vsum.step(4)
+        newton(m_ref,x_ref,nb,pb,sb,xb,between)
         tr=jnp.zeros((1,1),f32)
         for i in range(nblk):
             r=slice(i*RB,(i+1)*RB); tr=tr+diag_sum(x_ref[r,r])
@@ -674,12 +706,16 @@
             send_r.wait_send(); send_l.wait_send()
         def pk2(i,carry):
             uslots[i]=pack(m_ref[pl.ds(pl.multiple_of(i*24,8),24),:])
+            send_row(pc,pc.c*16+i,uslots.at[i],ur.at[b],us.at[i],ur_sem)
             return carry
         lax.fori_loop(0,16,pk2,0)
-        send_rows(pc,16,pc.c*16,uslots,ur.at[b],us,ur_sem,True)
+    @pl.when(jnp.logical_not(owner))
+    def _():
+        for i in (2,3,4): vsum.step(i)
+    vsum.step(5)
     r=lax.broadcasted_iota(jnp.int32,(D,128),1); j=lax.broadcasted_iota(jnp.int32,(D,128),0)
     pick=jnp.where((j==pc.me*24+r)&(r<24),1.0,0.0).astype(f32)
-    vg=lax.dot_general(va_ref[...],pick,(((1,),(0,)),((),())),precision=lax.Precision.HIGHEST,preferred_element_type=f32)[:12,:24]
+    vg=lax.dot_general(vcur[5],pick,(((1,),(0,)),((),())),precision=lax.Precision.HIGHEST,preferred_element_type=f32)[:12,:24]
     sn=BETA_TWO*sec_ref[...]+(1-BETA_TWO)*vg*vg
     vg_ref[...]=vg; sn_ref[...]=sn
     vn_ref[...]=vec_ref[...]-RATE_VEC*vg/(jnp.sqrt(sn)+1e-8)
@@ -696,18 +732,19 @@
     lax.fori_loop(0,NB,upd,0)
     @pl.when(owner)
     def _():
-        rcopy(gown_ref.at[:,pc.cols],gown_ref.at[:,pc.cols],es.at[3],er.at[3],pc.sib).wait_send()
+        swap().wait_send()
         send_rows(pc,32,0,slots,ggr.at[2*b+pc.c],gs,gr,False)
         send_rows(pc,16,pc.c*16,uslots,ur.at[b],us,ur_sem,False)
-
-def call_newton_step(gown,stat,left,right,mas,va,vec,sec):
+    vsum.done()
+
+def call_newton_step(gown,statl,statr,left,right,mas,va,vec,sec):
     V=pltpu.VMEM; S=jax.ShapeDtypeStruct
     B=pl.BlockSpec(memory_space=V); sem=pltpu.SemaphoreType.DMA
     rows=S((NB,24,D),f32); small=S((NB,24),f32)
-    return pl.pallas_call(newton_body,in_specs=[B]*8,out_specs=[B]*6,out_shape=[rows]*3+[small]*3,
-        scratch_shapes=[V((D,D),f32)]*2+[V((D,D),bf16)]*4+[V((32,48,HC),bf16),V((24,48,HC),bf16),V((16,48,HC),bf16),V((12,48,HC),bf16),V((D,D),bf16),V((D,D),bf16),V((2,8,128),f32),V((D,D),bf16),
-            sem((32,)),sem,sem((16,)),sem,sem((4,)),sem((4,))],
-        compiler_params=pltpu.CompilerParams(vmem_limit_bytes=62<<20,collective_id=2,has_side_effects=True))(gown,stat,left,right,mas,va,vec,sec)
+    return pl.pallas_call(newton_body,in_specs=[B]*9,out_specs=[B]*6,out_shape=[rows]*3+[small]*3,
+        scratch_shapes=[V((D,D),f32)]*2+[V((D,D),bf16)]*4+[V((32,48,HC),bf16),V((24,48,HC),bf16),V((16,48,HC),bf16),V((12,48,HC),bf16),V((D,D),bf16),V((D,D),bf16),V((2,8,128),f32),V((D,D),bf16),V((6,16,D),f32),V((5,16,D),f32),V((D,D),f32),
+            sem((32,)),sem,sem((16,)),sem,sem((4,)),sem((4,)),sem((5,)),sem((5,))],
+        compiler_params=pltpu.CompilerParams(vmem_limit_bytes=62<<20,collective_id=2,has_side_effects=True))(gown,statl,statr,left,right,mas,va,vec,sec)
 
 
 def place_params(pg_ref,p_ref):
@@ -755,9 +792,32 @@
     l=pltpu.roll(jnp.where(low,os[1],os[0]),64,1)
     ctx_ref[rows,cols]=(jnp.where(low,os[0],os[1])/l).astype(bf16)
 
+class StatMove:
+    def __init__(self,pc,src,dst,side,ss,rsem):
+        self.pc,self.src,self.dst,self.side,self.ss,self.rsem=pc,src,dst,side,ss,rsem
+    def move(self,i,start):
+        pc=self.pc
+        b=(i+pc.me)%NB
+        t=owner_of(b)
+        src,dst=self.src.at[b],self.dst.at[pc.me]
+        mine=(pc.chip==t)&(pc.c==self.side)
+        if start:
+            @pl.when(mine)
+            def _(): pltpu.make_async_copy(src,dst,self.rsem).start()
+        @pl.when(jnp.logical_not(mine))
+        def _():
+            d=rcopy(src,dst,self.ss.at[b],self.rsem,(t//2,(t%2)*2+self.side))
+            if start: d.start()
+            else: d.wait_send()
+    def done(self):
+        pc=self.pc
+        lax.fori_loop(0,NB,lambda i,c: (self.move(i,False),c)[1],0)
+        @pl.when((pc.xy<3)&(pc.c==self.side))
+        def _(): pltpu.make_async_copy(self.dst,self.dst,self.rsem).wait()
+
 AORDER=(0,1,2,3,4,8,5,9,6,10,7,11)
 TT=256
-def front_body(len_ref,x_ref,cot_ref,mas_ref,pv_ref,left_ref,right_ref,
+def front_body(len_ref,x_ref,cot_ref,mas_ref,pv_ref,left_ref,
                out_o,qa_o,ka_o,v_o,ctx_o,act_o,din_o,dffn_o,hlow_o,dz1_o,dctx_o,wq_o,vec_o,st_ref,
                w_ref,pg_ref,p_ref,sibm,q,k,v,ctx,doc,qa,ka,va,n1,r1,hlow,acc,act,gp,dffn,dctx,out,
                ss,rs,cs,cr,ts,tr,lsem,asem,osem):
@@ -777,25 +837,13 @@
         return Gather(pc,w_ref.at[g-1],ss.at[g],rs.at[g]).copies()
     NG=13
     def tick(t):
-        for s in range(5):
+        for s,d in ((0,-3),(1,0),(2,1),(3,2),(4,3)):
             if isinstance(t,int):
-                if 0<=t-s<NG and not (s==0 and t<4): group(t-s).step(s)
+                if 0<=t-d<NG and not (s==0 and t<1): group(t-d).step(s)
             else:
-                @pl.when(t-s<NG)
-                def _(): group(t-s).step(s)
-    def stat(i,start):
-        b=(i+pc.me)%NB
-        t=owner_of(b)
-        for side,ref in enumerate((left_ref,right_ref)):
-            mine=(pc.chip==t)&(pc.c==side)
-            d=rcopy(ref.at[b],st_ref.at[pc.me],ts.at[b*2+side],tr,(t//2,(t%2)*2+side))
-            if start:
-                @pl.when(mine)
-                def _(): pltpu.make_async_copy(ref.at[b],st_ref.at[pc.me],tr).start()
-            @pl.when(jnp.logical_not(mine))
-            def _():
-                if start: d.start()
-                else: d.wait_send()
+                @pl.when(t-d<NG)
+                def _(): group(t-d).step(s)
+    stats=StatMove(pc,left_ref,st_ref,0,ts,tr)
     copies=[]
     def away(src,dst):
         i=len(copies)
@@ -808,7 +856,7 @@
         group(i+1).step(0)
     other.wait_recv()
     assemble(range(3,12))
-    for t in range(1,5): tick(t)
+    for t in range(4): tick(t)
     place_params(pg_ref,p_ref)
     t_=lax.broadcasted_iota(jnp.int32,(PACK,128),0)
     end=jnp.int32(0); dd=jnp.zeros((PACK,128),jnp.int32)
@@ -817,7 +865,7 @@
         dd=dd+(t_>=end).astype(jnp.int32)
     doc[...]=dd
     for i,(o,b,dst) in enumerate(((q,0,None),(k,None,None),(v,1,v_o))):
-        tick(5+i)
+        tick(4+i)
         for tl in range(4):
             rows=pl.ds(tl*TT,TT)
             y=dot(x_ref[rows,:],W(i))
@@ -839,9 +887,7 @@
         @pl.when(b==1)
         def _():
             for c in pair_copies(p): c.start()
-            tick(8+p)
-        @pl.when(n%2==1)
-        def _(): stat(n//2,True)
+            tick(7+p)
         return carry
     lax.fori_loop(0,12,slot,0)
     away(ctx,ctx_o)
@@ -856,7 +902,6 @@
         hlow[rows,:]=(n*g1+s1).astype(bf16)
         return carry
     lax.fori_loop(0,4,out_proj,0)
-    tick(14)
     def chunk_copy(c):
         lane=pl.ds(pl.multiple_of(c*D,128),D)
         return pltpu.make_async_copy(act.at[:,lane],act_o.at[:,lane],osem.at[5,c])
@@ -876,11 +921,12 @@
             @pl.when(c>0)
             def _(): acc[rows,:]+=y
         chunk_copy(c).start()
-        @pl.when(c<2)
-        def _(): tick(15+c)
+        @pl.when(c<3)
+        def _(): tick(13+c)
+        @pl.when(c==2)
+        def _(): lax.fori_loop(0,NB,lambda i,a: (stats.move(i,True),a)[1],0)
         return carry
     lax.fori_loop(0,4,chunk,0)
-    lax.fori_loop(6,NB,lambda b,c: (stat(b,True),c)[1],0)
     away(hlow,hlow_o)
     pltpu.make_async_copy(cot_ref,out,lsem.at[20]).start()
     pltpu.make_async_copy(cot_ref,out,lsem.at[20]).wait()
@@ -929,24 +975,22 @@
     first.wait_send(); other.wait_send()
     group(0).done()
     lax.fori_loop(1,NG,lambda g,c: (group(g).done(),c)[1],0)
-    lax.fori_loop(0,NB,lambda b,c: (stat(b,False),c)[1],0)
-    @pl.when(pc.xy<3)
-    def _(): pltpu.make_async_copy(st_ref,st_ref,tr).wait()
-
-def call_front(lengths,x,cot,masters,pv,left,right):
+    stats.done()
+
+def call_front(lengths,x,cot,masters,pv,left):
     V=pltpu.VMEM; S=jax.ShapeDtypeStruct; A=pl.ANY
     B=lambda m: pl.BlockSpec(memory_space=m)
     sem=pltpu.SemaphoreType.DMA
     T=lambda w,d: S((PACK,w),d)
     return pl.pallas_call(front_body,
-        in_specs=[B(pltpu.SMEM),B(V),B(A),B(V),B(V),B(A),B(A)],
+        in_specs=[B(pltpu.SMEM),B(V),B(A),B(V),B(V),B(A)],
         out_specs=[B(A)]*12+[B(V),B(A)],
         out_shape=[T(D,bf16)]+[S((6,2,PACK,128),bf16)]*2+[T(D,bf16)]*2+[T(FF,bf16),T(FF,bf16),T(D,bf16),T(D,bf16),T(D,f32),T(D,bf16),S((3,4,4,MR,D),bf16),S((16,D),f32),S((32,24,D),f32)],
         scratch_shapes=[V((NB,4,4,MR,D),bf16),V((4,4,16,D),bf16),V((16,D),f32),V((NB,24,HC),f32)]+[V((PACK,D),bf16)]*4+
             [V((PACK,128),jnp.int32),V((2,2,PACK,128),bf16),V((2,2,PACK,128),bf16),V((2,PACK,128),bf16),V((PACK,D),f32),V((PACK,128),f32),V((PACK,D),bf16),V((PACK,D),f32),
              V((PACK,FF),bf16),V((PACK,FF),bf16),V((PACK,D),bf16),V((PACK,D),bf16),V((PACK,D),bf16),
-             sem((13,11)),sem((13,11)),sem((2,)),sem((2,)),sem((24,)),sem,sem((24,)),sem((2,2)),sem((6,4))],
-        compiler_params=pltpu.CompilerParams(vmem_limit_bytes=63<<20,collective_id=0,has_side_effects=True))(lengths,x,cot,masters,pv,left,right)
+             sem((13,11)),sem((13,11)),sem((2,)),sem((2,)),sem((NB,)),sem,sem((24,)),sem((2,2)),sem((6,4))],
+        compiler_params=pltpu.CompilerParams(vmem_limit_bytes=63<<20,collective_id=0,has_side_effects=True))(lengths,x,cot,masters,pv,left)
 
 
 NGR=12
@@ -1061,6 +1105,7 @@
         self.targets(g,wait)
 
 KB_=512
+PACE={1:(("step1",0),),4:(("step1",1),),5:(("step2",0),),7:(("step1",2),),8:(("step2",1),("step3",0))}
 def prepare_pair(p,v,ctx,do,doa,va):
     cols=pl.ds(pl.multiple_of(p*128,128),128)
     lane=lax.broadcasted_iota(jnp.int32,(256,128),1)
@@ -1101,11 +1146,11 @@
     dv_ref[rows,cols]=jnp.where(low,r[0][0],r[1][0]).astype(bf16)
     dk_ref[rows,cols]=jnp.where(low,r[0][1],r[1][1]).astype(bf16)
 
-def back_body(x_ref,qa_i,ka_i,v_i,ctx_i,do_i,act_i,din_i,dffn_i,hlow_i,dz1_i,wq_i,vec_ref,
-              ig_o,out_ref,vout_ref,gown_ref,*rest):
+def back_body(x_ref,qa_i,ka_i,v_i,ctx_i,do_i,act_i,din_i,dffn_i,hlow_i,dz1_i,wq_i,vec_ref,right_ref,
+              ig_o,out_ref,vcur,gown_ref,st_ref,*rest):
     R=dict(zip(SKEYS,rest[:len(SKEYS)]))
-    (g_ref,ctx,w_last,act,din,dffn,hlow,acc,qa,doa,ka,va,dqa,vcur,vbuf,
-     ss,rs,os_,orr,vs,vr,lsem,asem)=rest[len(SKEYS):]
+    (g_ref,ctx,w_last,act,din,dffn,hlow,acc,qa,doa,ka,va,dqa,
+     ss,rs,os_,orr,ts,tr,lsem,asem)=rest[len(SKEYS):]
     pc=Place()
     loads={}
     def load(name,src,dst):
@@ -1123,10 +1168,11 @@
     for c in pair_loads(0): c.start()
     greet_all(pc)
     gs=GroupSum(pc,g_ref,R,out_ref,gown_ref,ss,rs,os_,orr)
-    vsum=VecSum(pc,vcur,vbuf,vs,vr)
+    stats=StatMove(pc,right_ref,st_ref,1,ts,tr)
     def product(g,a,b):
         for r in range(4):
             g_ref[g,r]=dot(a[:,r*192:(r+1)*192],b,0,0).astype(bf16).reshape(4,MR,D)
+    lax.fori_loop(0,NB,lambda i,a: (stats.move(i,True),a)[1],0)
     loads["dffn"].wait()
     for i in range(9):
         c=i//2
@@ -1144,8 +1190,7 @@
             if c<2: load(f"din{c+2}",half(din_i,c+2),din.at[c%2])
         if i in late: load(*late[i])
         gs.step0(i)
-        if i>=1: gs.step1(i-1)
-    gs.step2(0)
+        for s,g in PACE.get(i,()): getattr(gs,s)(g)
     wrow=pl.ds(0,D)
     wdst=[din.at[1,wrow],hlow.at[wrow],w_last]
     for i in range(3): load(f"w{i}",wq_i.at[i],wdst[i])
@@ -1168,60 +1213,56 @@
             lane=pl.ds(pl.multiple_of(cc*HC,128),HC)
             for r in range(4):
                 g_ref[9+j,r,:,:,lane]=dot(x_ref[:,r*192:(r+1)*192],al,0,0).astype(bf16).reshape(4,MR,HC)
-            vcur[0,0:1,cols]=jnp.sum(q[:,cols].astype(f32),axis=0,keepdims=True)
-            vcur[0,1:2,cols]=jnp.sum(v[:,cols].astype(f32),axis=0,keepdims=True)
-        @pl.when(n==0)
-        def _(): gs.step1(8)
-        @pl.when(n<=9)
-        def _(): gs.step2(1+n)
-        @pl.when(n<=10)
-        def _(): gs.step3(n)
+            vcur[0:1,cols]=jnp.sum(q[:,cols].astype(f32),axis=0,keepdims=True)
+            vcur[1:2,cols]=jnp.sum(v[:,cols].astype(f32),axis=0,keepdims=True)
+        @pl.when((n<=6)|(n==8))
+        def _(): gs.step1(3+n-n//8)
+        @pl.when((n<=7)|(n==9))
+        def _(): gs.step2(2+n-n//9)
+        @pl.when((n<=8)|(n==10))
+        def _(): gs.step3(1+n-n//10)
         @pl.when(n>=1)
         def _(): gs.step4(n-1)
         @pl.when(n>=2)
         def _(): gs.step5(n-2)
-        @pl.when((n==4)|(n==8))
-        def _(): gs.step1(8+n//4)
         @pl.when((n==3)|(n==7))
         def _(): gs.step0(9+n//7)
         return carry
-    vcur[0]=vec_ref[...]
+    vcur[...]=vec_ref[...]
     lax.fori_loop(0,12,slot,0)
     gs.step0(11)
-    vsum.step(0)
     for i in range(3): loads[f"w{i}"].wait()
     def grad_tile(t):
         rows=pl.ds(t*256,256)
         a=acc[rows,:]
         for d,w in zip((q,k,v),wdst): a=a+dot(d[rows,:],w[...],1,1)
         acc[rows,:]=a
-    grad_tile(0);
-    gs.step5(10); gs.step1(11); vsum.step(1)
-    grad_tile(1); grad_tile(2); vsum.step(2)
-    gs.step2(11); grad_tile(3); vsum.step(3)
+    grad_tile(0)
+    gs.step5(10); gs.step1(11)
+    grad_tile(1); grad_tile(2)
+    gs.step2(11); grad_tile(3)
     away=pltpu.make_async_copy(acc,ig_o,lsem.at[31]); away.start()
-    gs.step3(11); vsum.step(4)
-    gs.step4(11); vsum.step(5)
+    gs.step3(11)
+    gs.step4(11)
     gs.step5(11)
-    vout_ref[...]=vcur[5]
-    vsum.done()
     lax.fori_loop(0,NGR,lambda g,c: (gs.done(g),c)[1],0)
     away.wait()
+    stats.done()
     @pl.when(pc.xy<3)
     def _(): pltpu.make_async_copy(gown_ref,gown_ref,orr).wait()
 
-def call_back(x,qa,ka,v,ctx,dctx,act,din,dffn,hlow,dz1,wq,vec):
+def call_back(x,qa,ka,v,ctx,dctx,act,din,dffn,hlow,dz1,wq,vec,right):
     V=pltpu.VMEM; S=jax.ShapeDtypeStruct; A=pl.ANY
     B=lambda m: pl.BlockSpec(memory_space=m)
     sem=pltpu.SemaphoreType.DMA
     T=V((PACK,D),bf16); H=V((2,PACK,128),bf16)
     return pl.pallas_call(back_body,
-        in_specs=[B(V)]+[B(A)]*11+[B(V)],
-        out_specs=[B(A),B(V),B(V),B(A)],
-        out_shape=[S((PACK,D),f32),S((NB,24,D),f32),S((16,D),f32),S((16,MR,HC),bf16)],
+        in_specs=[B(V)]+[B(A)]*11+[B(V),B(A)],
+        out_specs=[B(A),B(V),B(V),B(A),B(A)],
+        out_shape=[S((PACK,D),f32),S((NB,24,D),f32),S((16,D),f32),S((16,MR,HC),bf16),S((32,24,D),f32)],
         scratch_shapes=list(sum_scratch().values())+[V((NGR,4,4,MR,D),bf16),T,V((D,D),bf16)]+[V((2,PACK,D),bf16),V((2,PACK,D),bf16),T,T,V((PACK,D),f32)]+[V((2,2,PACK,128),bf16),H,V((2,2,PACK,128),bf16),H]+
-            [V((PACK,128),f32),V((6,16,D),f32),V((5,16,D),f32),sem((NGR,10)),sem((NGR,10)),sem((NGR,3)),sem,sem((5,)),sem((5,)),sem((32,)),sem((2,2))],
-        compiler_params=pltpu.CompilerParams(vmem_limit_bytes=63<<20,collective_id=1,has_side_effects=True))(x,qa,ka,v,ctx,dctx,act,din,dffn,hlow,dz1,wq,vec)
+            [V((PACK,128),f32),sem((NGR,10)),sem((NGR,10)),sem((NGR,3)),sem,sem((NB,)),sem,sem((32,)),sem((2,2))],
+        compiler_params=pltpu.CompilerParams(vmem_limit_bytes=63<<20,collective_id=1,has_side_effects=True))(x,qa,ka,v,ctx,dctx,act,din,dffn,hlow,dz1,wq,vec,right)
 
 
 def gather_rows(a):
@@ -1241,9 +1282,9 @@
 def on_slice(tokens,cotangent,lengths,masters,vectors,left,right,second):
     pv=jnp.pad(vectors,((0,4),(0,HC-24))).astype(bf16)
     lens=doc_lengths(lengths)
-    out,qa,ka,v,ctx,act,din,dffn,hlow,dz1,dctx,wq,vec,stat=call_front(lens,tokens,cotangent,masters,pv,left,right)
-    ig,grads,vec_all,gown=call_back(tokens,qa,ka,v,ctx,dctx,act,din,dffn,hlow,dz1,wq.reshape(3,D,D),vec)
-    ln,rn,mn,vg,sn,vn=call_newton_step(gown.reshape(D,HC),stat.reshape(D,D),left,right,masters,vec_all,vectors,second)
+    out,qa,ka,v,ctx,act,din,dffn,hlow,dz1,dctx,wq,vec,statl=call_front(lens,tokens,cotangent,masters,pv,left)
+    ig,grads,vec,gown,statr=call_back(tokens,qa,ka,v,ctx,dctx,act,din,dffn,hlow,dz1,wq.reshape(3,D,D),vec,right)
+    ln,rn,mn,vg,sn,vn=call_newton_step(gown.reshape(D,HC),statl.reshape(D,D),statr.reshape(D,D),left,right,masters,vec,vectors,second)
     return out,ig,grads,ln,rn,mn,vg,sn,vn
 
 def on_any(tokens,cotangent,lengths,masters,vectors,left,right,second):

time: 345 us -> 332 us (0.962)
  Pallas kernels: 326 us -> 312 us
    pallas_call x1, Pallas kernels: 140 us -> 120 us  [call_front(): pl.pallas_call(front_body, in_specs=[B(pltpu.SMEM), B(V), B(A), B(V), B(V...]
    pallas_call x2, Pallas kernels: 186 us -> 192 us  [the longest x1 124 us: call_back(): pl.pallas_call(back_body, in_specs=[B(V)] + [B(A)] * 11 + [B(V), B(A)], o...]
where the time goes in v1:
time: 332 us; the launch traced here: 325 us
  Pallas kernels  312 us (94%)
  local copies, waits for them, and re-layouts  11.5 us (3%)
    pallas_call x1, Pallas kernels, call_back(): pl.pallas_call(back_body, in_specs=[B(V)] + [B(A)] * 11 + [B(V), B(A)], o...  124 us
    pallas_call x1, Pallas kernels, call_front(): pl.pallas_call(front_body, in_specs=[B(pltpu.SMEM), B(V), B(A), B(V), B(V...  120 us
    pallas_call x1, Pallas kernels, call_newton_step(): pl.pallas_call(newton_body, in_specs=[B] * 9, out_specs=[B] * 6, out_shap...  68.1 us
    unnamed x29, local copies, waits for them, and re-layouts  10.4 us

profile of v1, /device:TPU:11, one launch (start us, length us, event | category | flops | bytes accessed | tf_op | source)
XLA Modules:
  0.0 325.3 jit_solution(17199555780482539596)
XLA Ops:
  0.6 0.0 copy-start
  0.7 0.7 copy-done
  1.3 0.5 constant_dynamic-slice_fusion.len_ref
  1.8 0.7 convert.4
  2.5 0.6 pad.5.pv_ref
  3.2 120.3 %shard_map.151 = (bf16[1024,768]{1,0:T(8,128)(2,1)}, bf16[6,2,1024,128]{3,2,1,0:T(8,128)(2,1)}, bf16[6,2,1024,128]{3,2,1,0:T(8,128)(2,1)}, bf16[1024,768]{1,0:T(...) custom-call(s32[1,8]{1,0:T(1,128)} %constant_dynamic-slice_fusion.le, ...), custom_call_target="tpu_custom_call" | custom-call | tf_op jit(solution)/shard_map/pallas_call | solution.py:985
  123.4 123.8 %shard_map.152 = (f32[1024,768]{1,0:T(8,128)}, f32[12,24,768]{2,1,0:T(8,128)}, f32[16,768]{1,0:T(8,128)}, bf16[16,48,384]{2,1,0:T(8,128)(2,1)}, f32[32,24,768]{2,1,0:T(8,128)}) custom-call(bf16[1024,768]{1,0:T(8,128)(2,1)} %x_ref.3, bf16[6,2,1024,128]{3,2,1,0:T(8,128)(2,1)} %get-tuple-element.35.qa_i, bf16[6,2,1024,128]{3,2,1,0:T(8,128)(2,1)} %get-tuple-element.36.ka_i, ...), custom_call_target="tpu_custom_call" | custom-call | tf_op jit(solution)/shard_map/pallas_call | solution.py:1259
  247.2 0.0 copy-start.2
  247.2 68.1 %shard_map.153 = (f32[12,24,768]{2,1,0:T(8,128)}, f32[12,24,768]{2,1,0:T(8,128)}, f32[12,24,768]{2,1,0:T(8,128)}, f32[12,24]{1,0:T(8,128)}, f32[12,24]{1,0:T(8,128)}, /*index=5*/f32[12,24]{1,0:T(8,128)}) custom-call(bf16[768,384]{1,0:T(8,128)(2,1)} %bitcast.7, f32[768,768]{1,0:T(8,128)} %bitcast.5, f32[768,768]{1,0:T(8,128)} %bitcast.6, ...), custom_call_target="tpu_custom_call" | custom-call | tf_op jit(solution)/shard_map/pallas_call | solution.py:744
  315.3 0.0 copy-start.1
  315.3 0.0 copy-done.2
  315.3 1.1 copy.26
  316.5 1.3 copy-done.1
  317.8 1.7 copy.27
  319.4 0.1 copy-done.3
  319.6 0.9 copy.28
  320.5 0.9 copy.29
  321.4 0.0 copy-done.5
  321.4 0.9 copy.30
  322.3 0.0 copy-done.4
  322.3 0.9 copy.31
  323.2 0.6 copy.32
  323.8 0.6 copy.33
  324.4 0.6 copy.34
  (11 shorter events, 0.0 us)
Async XLA Ops:
  0.6 0.7 copy-start
  247.2 68.1 %copy-start.2 = (bf16[1024,768]{1,0:T(8,128)(2,1)S(1)}, bf16[1024,768]{1,0:T(8,128)(2,1)}, u32[]{:S(2)}) copy-start(bf16[1024,768]{1,0:T(8,128)(2,1)} %get-tuple-element.68) | copy-start | bytes 4718596
  315.3 2.5 copy-start.1
  317.8 1.8 copy-start.3
  317.8 2.7 copy-start.6
  319.6 1.8 copy-start.5
  319.6 2.8 copy-start.4
  320.5 2.8 copy-start.9
  320.5 3.4 %copy-start.8 = (f32[12,24]{1,0:T(8,128)S(1)}, f32[12,24]{1,0:T(8,128)}, u32[]{:S(2)}) copy-start(f32[12,24]{1,0:T(8,128)} %get-tuple-element.75) | copy-start | bytes 3460
  320.5 4.0 %copy-start.7 = (f32[12,24]{1,0:T(8,128)S(1)}, f32[12,24]{1,0:T(8,128)}, u32[]{:S(2)}) copy-start(f32[12,24]{1,0:T(8,128)} %get-tuple-element.76) | copy-start | bytes 3460
